TPU v7x, 512 devices: a whole 4x8x8 slice. The times are simulated.
512 devices in a mesh: group: 8 (over z), dom: 64 (over x, y, core).
Axes of the slice: x: 4, y: 8, z: 8, core: 2. Of those that a mesh axis runs over, the one named last changes fastest.
Arguments:
- basis_start: bfloat16 [8, 2304, 32, 128], P('group', 'dom'), may hold values from -4096 to 4096, as said below
- templates: bfloat16 [64, 128, 128], replicated, may hold values from -0.1875 to 0.1875
- template_ids: int32 [8, 2304, 7], P('group', 'dom'), may hold values from 0 to 63
- live_columns: int32 [64], P('dom'), may hold values from 4 to 36, as said below
- face_refs: int32 [2304, 4], P('dom'), may hold values from -1 to 83, as said below
- send_lists: int32 [64, 8, 6], P('dom'), may hold values from -1 to 35, as said below
Outputs:
- basis_q: bfloat16 [8, 2304, 96, 128], P('group', 'dom')
- r_factor: float32 [96, 96], replicated
Inputs may be any that keep to these rules, and one draw needn't show every extreme that they name: `basis_start`: standard deviations vary by element, by right-hand side and by slab and piece. Piece d's live columns are slots 0 to live_columns[d] - 1; the pieces and all lists are the same for every slab. `face_refs`: every entry of a live column is -1 (no neighbour) or a slot of the piece's own 36 columns followed by 8 blocks of 6 received slots; own slots are live, received slots are filled ones of the source piece's list. Rows of slots that are not live are -1. `send_lists`: row (d, k) lists live columns of piece d in rising order, then -1; rows toward a position off the grid of pieces are all -1; some row is full.
All inputs are finite; a program needn't handle non-finite values.
Results may differ from a plain program's by a relative error of at most 0.014.
Values may be sent and summed in bfloat16 or wider, within the bound.
A program may use at most 64 MiB of HBM per device.

v0:
```python
import math

import jax
import jax.numpy as jnp
from jax import lax
from jax.sharding import PartitionSpec as P

DIRECTIONS = ((-1, -1), (-1, 0), (-1, 1), (0, -1), (0, 1), (1, -1), (1, 0), (1, 1))


def from_behind(value, axis, steps):
    count = lax.axis_size(axis)
    leading, last = (max(0, -steps), min(count, count - steps))
    return lax.ppermute(value, axis, [(source, source + steps) for source in range(leading, last)])


def extended(shard, sides, width):
    for axis, dim in sides:
        peers, length = (lax.axis_size(axis), shard.shape[dim])
        up = [(i, (i + 1) % peers) for i in range(peers - 1)]
        down = [(j, i) for i, j in up]
        last = lax.slice_in_dim(shard, length - width, length, axis=dim)
        leading = lax.slice_in_dim(shard, 0, width, axis=dim)
        before = lax.ppermute(last, axis, up)
        after = lax.ppermute(leading, axis, down)
        shard = jnp.concatenate([before, shard, after], axis=dim)
    return shard


def body(basis_start, templates, template_ids, live_columns, face_refs, send_lists):
    layer_count, column_cap, rhs_count, dof_count = basis_start.shape
    grid_side = math.isqrt(lax.axis_size("dom"))
    halo_cap = send_lists.shape[2]
    live_mask = jnp.arange(column_cap, dtype=jnp.int32) < live_columns[0]
    masked_start = jnp.where(
        live_mask[None, :, None, None], basis_start, jnp.zeros((), jnp.bfloat16)
    )
    send_rows = send_lists[0]
    send_valid = (send_rows >= 0).reshape(-1)
    send_index = jnp.maximum(send_rows, 0).reshape(-1)
    valid_ref = face_refs >= 0
    ref_index = jnp.maximum(face_refs, 0).reshape(-1)
    layer_weights = [templates[template_ids[0]]]

    def outgoing(vector):
        packets = vector[:, send_index]
        packets = jnp.where(send_valid[None, :, None, None], packets, jnp.zeros((), jnp.bfloat16))
        return packets.reshape(layer_count, 8, halo_cap, rhs_count, dof_count)

    def ghosts(vector):
        packets = outgoing(vector)
        blocks = []
        for which, (step_x, step_y) in enumerate(DIRECTIONS):
            blocks.append(from_behind(packets[:, which], "dom", step_x * grid_side + step_y))
        return jnp.stack(blocks, 1)

    def operate(vector):
        ghost_rows = ghosts(vector).reshape(layer_count, 8 * halo_cap, rhs_count, dof_count)
        lookup = jnp.concatenate([vector, ghost_rows], 1)
        padded = extended(vector, (("group", 0),), 1)
        beside = lookup[:, ref_index].reshape(layer_count, column_cap, 4, rhs_count, dof_count)
        beside = jnp.where(valid_ref[None, :, :, None, None], beside, jnp.zeros((), jnp.bfloat16))
        operands = jnp.concatenate([jnp.stack([vector[0], padded[0], padded[2]], 1), beside[0]], 1)
        results = [
            jnp.einsum(
                "cfij,cfrj->cri", layer_weights[0], operands, preferred_element_type=jnp.float32
            )
        ]
        return jnp.stack(results, 0)

    first_power = operate(masked_start).astype(jnp.bfloat16)
    second_power = operate(first_power).astype(jnp.bfloat16)
    stacked = jnp.concatenate([masked_start, first_power, second_power], 2)
    local_gram = jnp.einsum("zcpd,zcqd->pq", stacked, stacked, preferred_element_type=jnp.float32)
    gram_matrix = lax.psum(local_gram, ("group", "dom"))
    rows_total = (
        layer_count * column_cap * dof_count * lax.axis_size("group") * lax.axis_size("dom")
    )
    gram_matrix = gram_matrix / rows_total
    lower_factor = jnp.linalg.cholesky(gram_matrix)
    basis_width = gram_matrix.shape[0]
    inverse = lax.linalg.triangular_solve(
        lower_factor, jnp.eye(basis_width, dtype=gram_matrix.dtype), left_side=True, lower=True
    )
    inverse_high = inverse.astype(jnp.bfloat16)
    inverse_low = (inverse - inverse_high.astype(jnp.float32)).astype(jnp.bfloat16)
    basis_q = jnp.einsum("zcpd,qp->zcqd", stacked, inverse_high, preferred_element_type=jnp.float32)
    basis_q = basis_q + jnp.einsum(
        "zcpd,qp->zcqd", stacked, inverse_low, preferred_element_type=jnp.float32
    )
    return (basis_q.astype(jnp.bfloat16), lower_factor.T)


def solution(mesh):
    return jax.shard_map(
        body,
        mesh=mesh,
        in_specs=(
            P("group", "dom", None, None),
            P(),
            P("group", "dom", None),
            P("dom"),
            P("dom", None),
            P("dom", None, None),
        ),
        out_specs=(P("group", "dom", None, None), P()),
        check_vma=False,
    )
```

profile of v0, /device:TPU:1, one launch (start us, length us, event | category | flops | bytes accessed | tf_op | source)
XLA Modules:
  0.0 253.8 jit_solution(16788577126682859798)
XLA Ops:
  2.6 5.5 %collective-permute-start = (bf16[1,36,32,128]{3,2,1,0:T(8,128)(2,1)S(1)}, bf16[1,36,32,128]{3,2,1,0:T(8,128)(2,1)}, u32[]{:S(2)}, u32[]{:S(2)}) collective-permute-start(bf16[1,36,32,128]{3,2,1,0:T(8,128)(2,1)S(1)} %broadcast_select_fusion.4), channel_id=1, source_target_pairs={{0,64},{64,128},{128,192},{192,256},{256,320},{320,384},{384,448},... | collective-permute-start | bytes 884744 | tf_op jit(solution)/shard_map/ppermute | solution.py:24
  16.8 8.6 %gather_fusion.2 = bf16[252,128,128]{2,1,0:T(8,128)(2,1)} fusion(bf16[64,128,128]{2,1,0:T(8,128)(2,1)S(1)} %copy-done, s32[1024]{0:T(1024)S(1)} %get-tuple-element.24), kind=kCustom, calls=%fused_computation.2 | custom fusion | bytes 16516080 | tf_op jit(solution)/shard_map/gather | solution.py:43
  25.4 5.2 %collective-permute-start.5 = (bf16[1,6,32,128]{3,2,1,0:T(8,128)(2,1)S(1)}, bf16[1,6,32,128]{3,2,1,0:T(8,128)(2,1)S(1)}, u32[]{:S(2)}, u32[]{:S(2)}) collective-permute-start(bf16[1,6,32,128]{3,2,1,0:T(8,128)(2,1)S(1)} %get-tuple-element.18), channel_id=1, source_target_pairs={{1,0},{2,1},{3,2},{4,3},{5,4},{6,5},{7,6},{8,7},{9,8},{10,9},{11,1... | collective-permute-start | bytes 147464 | tf_op jit(solution)/shard_map/ppermute | solution.py:14
  30.7 1.9 collective-permute-start.6
  32.6 9.4 %collective-permute-start.7 = (bf16[1,6,32,128]{3,2,1,0:T(8,128)(2,1)S(1)}, bf16[1,6,32,128]{3,2,1,0:T(8,128)(2,1)S(1)}, u32[]{:S(2)}, u32[]{:S(2)}) collective-permute-start(bf16[1,6,32,128]{3,2,1,0:T(8,128)(2,1)S(1)} %get-tuple-element.16), channel_id=1, source_target_pairs={{0,7},{1,8},{2,9},{3,10},{4,11},{5,12},{6,13},{7,14},{8,15},{9,16}... | collective-permute-start | bytes 147464 | tf_op jit(solution)/shard_map/ppermute | solution.py:14
  42.1 8.6 %collective-permute-start.8 = (bf16[1,6,32,128]{3,2,1,0:T(8,128)(2,1)S(1)}, bf16[1,6,32,128]{3,2,1,0:T(8,128)(2,1)S(1)}, u32[]{:S(2)}, u32[]{:S(2)}) collective-permute-start(bf16[1,6,32,128]{3,2,1,0:T(8,128)(2,1)S(1)} %get-tuple-element.15), channel_id=1, source_target_pairs={{0,8},{1,9},{2,10},{3,11},{4,12},{5,13},{6,14},{7,15},{8,16},{9,17... | collective-permute-start | bytes 147464 | tf_op jit(solution)/shard_map/ppermute | solution.py:14
  50.7 6.5 %collective-permute-start.9 = (bf16[1,6,32,128]{3,2,1,0:T(8,128)(2,1)S(1)}, bf16[1,6,32,128]{3,2,1,0:T(8,128)(2,1)S(1)}, u32[]{:S(2)}, u32[]{:S(2)}) collective-permute-start(bf16[1,6,32,128]{3,2,1,0:T(8,128)(2,1)S(1)} %get-tuple-element.14), channel_id=1, source_target_pairs={{0,9},{1,10},{2,11},{3,12},{4,13},{5,14},{6,15},{7,16},{8,17},{9,1... | collective-permute-start | bytes 147464 | tf_op jit(solution)/shard_map/ppermute | solution.py:14
  57.3 2.3 collective-permute-done.9
  59.7 1.9 gather_fusion.1
  61.7 1.5 broadcast_select_fusion.1
  63.2 6.5 %fusion.23 = bf16[36,32,128]{2,1,0:T(8,128)(2,1)S(1)} fusion(bf16[36,7,128,128]{3,2,1,0:T(8,128)(2,1)} %bitcast.148, bf16[36,4,32,128]{3,2,1,0:T(8,128)(2,1)S(1)} %broadcast_select_fusion.1, bf16[36,1,32,128]{3,2,1,0:T(8,128)(2,1)} %bitcast.6, bf16[36,1,32,128]{3,2,1,0:T(8,128)(2,1)} %bitcast.4, bf16[36,1,32,128]{3,2,1,0:T(8,128)(2,1)S(1)} %fusion.46), kind=kOutput, calls=%fused_computation.25 | convolution fusion | flops 267485184 | bytes 10616832 | tf_op jit(solution)/shard_map/cfij,cfrj->cri/dot_general | solution.py:65
  71.8 5.0 %collective-permute-start.10 = (bf16[1,36,32,128]{3,2,1,0:T(8,128)(2,1)S(1)}, bf16[1,36,32,128]{3,2,1,0:T(8,128)(2,1)}, u32[]{:S(2)}, u32[]{:S(2)}) collective-permute-start(bf16[1,36,32,128]{3,2,1,0:T(8,128)(2,1)S(1)} %bitcast.150), channel_id=1, source_target_pairs={{0,64},{64,128},{128,192},{192,256},{256,320},{320,384},{384,448},... | collective-permute-start | bytes 884744 | tf_op jit(solution)/shard_map/ppermute | solution.py:24
  80.7 2.6 %collective-permute-start.15 = (bf16[1,6,32,128]{3,2,1,0:T(8,128)(2,1)S(1)}, bf16[1,6,32,128]{3,2,1,0:T(8,128)(2,1)S(1)}, u32[]{:S(2)}, u32[]{:S(2)}) collective-permute-start(bf16[1,6,32,128]{3,2,1,0:T(8,128)(2,1)S(1)} %get-tuple-element.10), channel_id=1, source_target_pairs={{1,0},{2,1},{3,2},{4,3},{5,4},{6,5},{7,6},{8,7},{9,8},{10,9},{11,1... | collective-permute-start | bytes 147464 | tf_op jit(solution)/shard_map/ppermute | solution.py:14
  83.3 5.1 %collective-permute-done.13 = bf16[1,6,32,128]{3,2,1,0:T(8,128)(2,1)S(1)} collective-permute-done((bf16[1,6,32,128]{3,2,1,0:T(8,128)(2,1)S(1)}, bf16[1,6,32,128]{3,2,1,0:T(8,128)(2,1)S(1)}, u32[]{:S(2)}, u32[]{:S(2)}) %collective-permute-start.13) | collective-permute-done | bytes 49184 | tf_op jit(solution)/shard_map/ppermute | solution.py:14
  88.4 5.5 %collective-permute-start.16 = (bf16[1,6,32,128]{3,2,1,0:T(8,128)(2,1)S(1)}, bf16[1,6,32,128]{3,2,1,0:T(8,128)(2,1)S(1)}, u32[]{:S(2)}, u32[]{:S(2)}) collective-permute-start(bf16[1,6,32,128]{3,2,1,0:T(8,128)(2,1)S(1)} %get-tuple-element.9), channel_id=1, source_target_pairs={{0,1},{1,2},{2,3},{3,4},{4,5},{5,6},{6,7},{7,8},{8,9},{9,10},{10,1... | collective-permute-start | bytes 147464 | tf_op jit(solution)/shard_map/ppermute | solution.py:14
  94.0 4.3 %collective-permute-start.17 = (bf16[1,6,32,128]{3,2,1,0:T(8,128)(2,1)S(1)}, bf16[1,6,32,128]{3,2,1,0:T(8,128)(2,1)S(1)}, u32[]{:S(2)}, u32[]{:S(2)}) collective-permute-start(bf16[1,6,32,128]{3,2,1,0:T(8,128)(2,1)S(1)} %get-tuple-element.8), channel_id=1, source_target_pairs={{0,7},{1,8},{2,9},{3,10},{4,11},{5,12},{6,13},{7,14},{8,15},{9,16}... | collective-permute-start | bytes 147464 | tf_op jit(solution)/shard_map/ppermute | solution.py:14
  98.3 6.4 %collective-permute-start.18 = (bf16[1,6,32,128]{3,2,1,0:T(8,128)(2,1)S(1)}, bf16[1,6,32,128]{3,2,1,0:T(8,128)(2,1)S(1)}, u32[]{:S(2)}, u32[]{:S(2)}) collective-permute-start(bf16[1,6,32,128]{3,2,1,0:T(8,128)(2,1)S(1)} %get-tuple-element.7), channel_id=1, source_target_pairs={{0,8},{1,9},{2,10},{3,11},{4,12},{5,13},{6,14},{7,15},{8,16},{9,17... | collective-permute-start | bytes 147464 | tf_op jit(solution)/shard_map/ppermute | solution.py:14
  104.8 9.7 %collective-permute-start.19 = (bf16[1,6,32,128]{3,2,1,0:T(8,128)(2,1)S(1)}, bf16[1,6,32,128]{3,2,1,0:T(8,128)(2,1)S(1)}, u32[]{:S(2)}, u32[]{:S(2)}) collective-permute-start(bf16[1,6,32,128]{3,2,1,0:T(8,128)(2,1)S(1)} %get-tuple-element.6), channel_id=1, source_target_pairs={{0,9},{1,10},{2,11},{3,12},{4,13},{5,14},{6,15},{7,16},{8,17},{9,1... | collective-permute-start | bytes 147464 | tf_op jit(solution)/shard_map/ppermute | solution.py:14
  115.8 1.9 gather_fusion.4
  117.7 1.5 broadcast_select_fusion
  119.2 6.5 %fusion.29 = bf16[1,36,32,128]{3,2,1,0:T(8,128)(2,1)S(1)} fusion(bf16[36,7,128,128]{3,2,1,0:T(8,128)(2,1)} %bitcast.149, bf16[36,4,32,128]{3,2,1,0:T(8,128)(2,1)S(1)} %broadcast_select_fusion, bf16[36,1,32,128]{3,2,1,0:T(8,128)(2,1)} %bitcast.39, bf16[36,1,32,128]{3,2,1,0:T(8,128)(2,1)} %bitcast.38, bf16[36,1,32,128]{3,2,1,0:T(8,128)(2,1)S(1)} %bitcast.153), kind=kOutput, calls=%fused_computation.29 | convolution fusion | flops 267485184 | bytes 10616832 | tf_op jit(solution)/shard_map/cfij,cfrj->cri/dot_general | solution.py:65
  126.1 107.4 %psum.7 = f32[96,96]{0,1:T(8,128)S(1)} all-reduce(f32[96,96]{0,1:T(8,128)S(1)} %convolution_bitcast_fusion), channel_id=1, replica_groups=mesh['group'=8,'dom'=64] {'group','dom'}, use_global_device_ids=true, to_apply=%region_0.1 | all-reduce | flops 9216 | bytes 73728 | tf_op jit(solution)/shard_map/psum | solution.py:75
  233.7 8.8 %cholesky.17 = f32[96,96]{1,0:T(8,128)S(1)} custom-call(f32[96,96]{1,0:T(8,128)S(1)} %fusion.34), custom_call_target="Cholesky" | custom-call | tf_op jit(solution)/shard_map/jit(cholesky)/cholesky | solution.py:80
  243.8 7.4 %custom-call.6 = f32[1,96,96]{1,2,0:T(8,128)S(1)} custom-call(f32[1,96,96]{2,1,0:T(8,128)S(1)} %get-tuple-element.23), custom_call_target="InvertDiagBlocksLowerTriangular" | custom-call | tf_op jit(solution)/shard_map/triangular_solve | solution.py:82
  (88 shorter events, 21.5 us)
Async XLA Ops:
  0.6 16.2 %copy-start = (bf16[64,128,128]{2,1,0:T(8,128)(2,1)S(1)}, bf16[64,128,128]{2,1,0:T(8,128)(2,1)}, u32[]{:S(2)}) copy-start(bf16[64,128,128]{2,1,0:T(8,128)(2,1)} %param.7) | copy-start | bytes 6291460
  1.5 14.6 %copy-start.2 = (s32[36,4]{0,1:T(4,128)S(1)}, s32[36,4]{0,1:T(4,128)}, u32[]{:S(2)}) copy-start(s32[36,4]{0,1:T(4,128)} %param.10) | copy-start | bytes 1732
  1.5 14.7 %copy-start.1 = (bf16[1,36,32,128]{3,2,1,0:T(8,128)(2,1)S(1)}, bf16[1,36,32,128]{3,2,1,0:T(8,128)(2,1)}, u32[]{:S(2)}) copy-start(bf16[1,36,32,128]{3,2,1,0:T(8,128)(2,1)} %param.6) | copy-start | bytes 884740
  2.6 13.6 %copy-start.3 = (s32[1,36,7]{1,0,2:T(1,128)S(1)}, s32[1,36,7]{1,0,2:T(1,128)}, u32[]{:S(2)}) copy-start(s32[1,36,7]{1,0,2:T(1,128)} %param.8) | copy-start | bytes 3028
  2.6 60.5 %collective-permute-start = (bf16[1,36,32,128]{3,2,1,0:T(8,128)(2,1)S(1)}, bf16[1,36,32,128]{3,2,1,0:T(8,128)(2,1)}, u32[]{:S(2)}, u32[]{:S(2)}) collective-permute-start(bf16[1,36,32,128]{3,2,1,0:T(8,128)(2,1)S(1)} %broadcast_select_fusion.4), channel_id=1, source_target_pairs={{0,64},{64,128},{128,192},{192,256},{256,320},{320,384},{384,448},... | collective-permute-start | bytes 884744 | tf_op jit(solution)/shard_map/ppermute | solution.py:24
  8.2 55.0 %collective-permute-start.1 = (bf16[1,36,32,128]{3,2,1,0:T(8,128)(2,1)S(1)}, bf16[1,36,32,128]{3,2,1,0:T(8,128)(2,1)}, u32[]{:S(2)}, u32[]{:S(2)}) collective-permute-start(bf16[1,36,32,128]{3,2,1,0:T(8,128)(2,1)S(1)} %broadcast_select_fusion.4), channel_id=1, source_target_pairs={{64,0},{128,64},{192,128},{256,192},{320,256},{384,320},{448,384},... | collective-permute-start | bytes 884744 | tf_op jit(solution)/shard_map/ppermute | solution.py:25
  12.2 13.2 %collective-permute-start.2 = (bf16[1,6,32,128]{3,2,1,0:T(8,128)(2,1)S(1)}, bf16[1,6,32,128]{3,2,1,0:T(8,128)(2,1)S(1)}, u32[]{:S(2)}, u32[]{:S(2)}) collective-permute-start(bf16[1,6,32,128]{3,2,1,0:T(8,128)(2,1)S(1)} %get-tuple-element.21), channel_id=1, source_target_pairs={{9,0},{10,1},{11,2},{12,3},{13,4},{14,5},{15,6},{16,7},{17,8},{18,... | collective-permute-start | bytes 147464 | tf_op jit(solution)/shard_map/ppermute | solution.py:14
  13.5 17.2 %collective-permute-start.3 = (bf16[1,6,32,128]{3,2,1,0:T(8,128)(2,1)S(1)}, bf16[1,6,32,128]{3,2,1,0:T(8,128)(2,1)S(1)}, u32[]{:S(2)}, u32[]{:S(2)}) collective-permute-start(bf16[1,6,32,128]{3,2,1,0:T(8,128)(2,1)S(1)} %get-tuple-element.20), channel_id=1, source_target_pairs={{8,0},{9,1},{10,2},{11,3},{12,4},{13,5},{14,6},{15,7},{16,8},{17,9... | collective-permute-start | bytes 147464 | tf_op jit(solution)/shard_map/ppermute | solution.py:14
  14.8 17.8 %collective-permute-start.4 = (bf16[1,6,32,128]{3,2,1,0:T(8,128)(2,1)S(1)}, bf16[1,6,32,128]{3,2,1,0:T(8,128)(2,1)S(1)}, u32[]{:S(2)}, u32[]{:S(2)}) collective-permute-start(bf16[1,6,32,128]{3,2,1,0:T(8,128)(2,1)S(1)} %get-tuple-element.19), channel_id=1, source_target_pairs={{7,0},{8,1},{9,2},{10,3},{11,4},{12,5},{13,6},{14,7},{15,8},{16,9}... | collective-permute-start | bytes 147464 | tf_op jit(solution)/shard_map/ppermute | solution.py:14
  25.4 16.7 %collective-permute-start.5 = (bf16[1,6,32,128]{3,2,1,0:T(8,128)(2,1)S(1)}, bf16[1,6,32,128]{3,2,1,0:T(8,128)(2,1)S(1)}, u32[]{:S(2)}, u32[]{:S(2)}) collective-permute-start(bf16[1,6,32,128]{3,2,1,0:T(8,128)(2,1)S(1)} %get-tuple-element.18), channel_id=1, source_target_pairs={{1,0},{2,1},{3,2},{4,3},{5,4},{6,5},{7,6},{8,7},{9,8},{10,9},{11,1... | collective-permute-start | bytes 147464 | tf_op jit(solution)/shard_map/ppermute | solution.py:14
  30.7 20.0 %collective-permute-start.6 = (bf16[1,6,32,128]{3,2,1,0:T(8,128)(2,1)S(1)}, bf16[1,6,32,128]{3,2,1,0:T(8,128)(2,1)S(1)}, u32[]{:S(2)}, u32[]{:S(2)}) collective-permute-start(bf16[1,6,32,128]{3,2,1,0:T(8,128)(2,1)S(1)} %get-tuple-element.17), channel_id=1, source_target_pairs={{0,1},{1,2},{2,3},{3,4},{4,5},{5,6},{6,7},{7,8},{8,9},{9,10},{10,1... | collective-permute-start | bytes 147464 | tf_op jit(solution)/shard_map/ppermute | solution.py:14
  32.6 24.6 %collective-permute-start.7 = (bf16[1,6,32,128]{3,2,1,0:T(8,128)(2,1)S(1)}, bf16[1,6,32,128]{3,2,1,0:T(8,128)(2,1)S(1)}, u32[]{:S(2)}, u32[]{:S(2)}) collective-permute-start(bf16[1,6,32,128]{3,2,1,0:T(8,128)(2,1)S(1)} %get-tuple-element.16), channel_id=1, source_target_pairs={{0,7},{1,8},{2,9},{3,10},{4,11},{5,12},{6,13},{7,14},{8,15},{9,16}... | collective-permute-start | bytes 147464 | tf_op jit(solution)/shard_map/ppermute | solution.py:14
  42.1 15.2 %collective-permute-start.8 = (bf16[1,6,32,128]{3,2,1,0:T(8,128)(2,1)S(1)}, bf16[1,6,32,128]{3,2,1,0:T(8,128)(2,1)S(1)}, u32[]{:S(2)}, u32[]{:S(2)}) collective-permute-start(bf16[1,6,32,128]{3,2,1,0:T(8,128)(2,1)S(1)} %get-tuple-element.15), channel_id=1, source_target_pairs={{0,8},{1,9},{2,10},{3,11},{4,12},{5,13},{6,14},{7,15},{8,16},{9,17... | collective-permute-start | bytes 147464 | tf_op jit(solution)/shard_map/ppermute | solution.py:14
  50.7 9.0 %collective-permute-start.9 = (bf16[1,6,32,128]{3,2,1,0:T(8,128)(2,1)S(1)}, bf16[1,6,32,128]{3,2,1,0:T(8,128)(2,1)S(1)}, u32[]{:S(2)}, u32[]{:S(2)}) collective-permute-start(bf16[1,6,32,128]{3,2,1,0:T(8,128)(2,1)S(1)} %get-tuple-element.14), channel_id=1, source_target_pairs={{0,9},{1,10},{2,11},{3,12},{4,13},{5,14},{6,15},{7,16},{8,17},{9,1... | collective-permute-start | bytes 147464 | tf_op jit(solution)/shard_map/ppermute | solution.py:14
  70.5 10.2 %collective-permute-start.12 = (bf16[1,6,32,128]{3,2,1,0:T(8,128)(2,1)S(1)}, bf16[1,6,32,128]{3,2,1,0:T(8,128)(2,1)S(1)}, u32[]{:S(2)}, u32[]{:S(2)}) collective-permute-start(bf16[1,6,32,128]{3,2,1,0:T(8,128)(2,1)S(1)} %get-tuple-element.13), channel_id=1, source_target_pairs={{9,0},{10,1},{11,2},{12,3},{13,4},{14,5},{15,6},{16,7},{17,8},{18,... | collective-permute-start | bytes 147464 | tf_op jit(solution)/shard_map/ppermute | solution.py:14
  71.8 47.4 %collective-permute-start.10 = (bf16[1,36,32,128]{3,2,1,0:T(8,128)(2,1)S(1)}, bf16[1,36,32,128]{3,2,1,0:T(8,128)(2,1)}, u32[]{:S(2)}, u32[]{:S(2)}) collective-permute-start(bf16[1,36,32,128]{3,2,1,0:T(8,128)(2,1)S(1)} %bitcast.150), channel_id=1, source_target_pairs={{0,64},{64,128},{128,192},{192,256},{256,320},{320,384},{384,448},... | collective-permute-start | bytes 884744 | tf_op jit(solution)/shard_map/ppermute | solution.py:24
  76.8 42.4 %collective-permute-start.11 = (bf16[1,36,32,128]{3,2,1,0:T(8,128)(2,1)S(1)}, bf16[1,36,32,128]{3,2,1,0:T(8,128)(2,1)}, u32[]{:S(2)}, u32[]{:S(2)}) collective-permute-start(bf16[1,36,32,128]{3,2,1,0:T(8,128)(2,1)S(1)} %bitcast.151), channel_id=1, source_target_pairs={{64,0},{128,64},{192,128},{256,192},{320,256},{384,320},{448,384},... | collective-permute-start | bytes 884744 | tf_op jit(solution)/shard_map/ppermute | solution.py:25
  78.1 10.4 %collective-permute-start.13 = (bf16[1,6,32,128]{3,2,1,0:T(8,128)(2,1)S(1)}, bf16[1,6,32,128]{3,2,1,0:T(8,128)(2,1)S(1)}, u32[]{:S(2)}, u32[]{:S(2)}) collective-permute-start(bf16[1,6,32,128]{3,2,1,0:T(8,128)(2,1)S(1)} %get-tuple-element.12), channel_id=1, source_target_pairs={{8,0},{9,1},{10,2},{11,3},{12,4},{13,5},{14,6},{15,7},{16,8},{17,9... | collective-permute-start | bytes 147464 | tf_op jit(solution)/shard_map/ppermute | solution.py:14
  79.4 14.6 %collective-permute-start.14 = (bf16[1,6,32,128]{3,2,1,0:T(8,128)(2,1)S(1)}, bf16[1,6,32,128]{3,2,1,0:T(8,128)(2,1)S(1)}, u32[]{:S(2)}, u32[]{:S(2)}) collective-permute-start(bf16[1,6,32,128]{3,2,1,0:T(8,128)(2,1)S(1)} %get-tuple-element.11), channel_id=1, source_target_pairs={{7,0},{8,1},{9,2},{10,3},{11,4},{12,5},{13,6},{14,7},{15,8},{16,9}... | collective-permute-start | bytes 147464 | tf_op jit(solution)/shard_map/ppermute | solution.py:14
  80.7 17.7 %collective-permute-start.15 = (bf16[1,6,32,128]{3,2,1,0:T(8,128)(2,1)S(1)}, bf16[1,6,32,128]{3,2,1,0:T(8,128)(2,1)S(1)}, u32[]{:S(2)}, u32[]{:S(2)}) collective-permute-start(bf16[1,6,32,128]{3,2,1,0:T(8,128)(2,1)S(1)} %get-tuple-element.10), channel_id=1, source_target_pairs={{1,0},{2,1},{3,2},{4,3},{5,4},{6,5},{7,6},{8,7},{9,8},{10,9},{11,1... | collective-permute-start | bytes 147464 | tf_op jit(solution)/shard_map/ppermute | solution.py:14
  88.4 16.4 %collective-permute-start.16 = (bf16[1,6,32,128]{3,2,1,0:T(8,128)(2,1)S(1)}, bf16[1,6,32,128]{3,2,1,0:T(8,128)(2,1)S(1)}, u32[]{:S(2)}, u32[]{:S(2)}) collective-permute-start(bf16[1,6,32,128]{3,2,1,0:T(8,128)(2,1)S(1)} %get-tuple-element.9), channel_id=1, source_target_pairs={{0,1},{1,2},{2,3},{3,4},{4,5},{5,6},{6,7},{7,8},{8,9},{9,10},{10,1... | collective-permute-start | bytes 147464 | tf_op jit(solution)/shard_map/ppermute | solution.py:14
  94.0 20.6 %collective-permute-start.17 = (bf16[1,6,32,128]{3,2,1,0:T(8,128)(2,1)S(1)}, bf16[1,6,32,128]{3,2,1,0:T(8,128)(2,1)S(1)}, u32[]{:S(2)}, u32[]{:S(2)}) collective-permute-start(bf16[1,6,32,128]{3,2,1,0:T(8,128)(2,1)S(1)} %get-tuple-element.8), channel_id=1, source_target_pairs={{0,7},{1,8},{2,9},{3,10},{4,11},{5,12},{6,13},{7,14},{8,15},{9,16}... | collective-permute-start | bytes 147464 | tf_op jit(solution)/shard_map/ppermute | solution.py:14
  98.3 16.2 %collective-permute-start.18 = (bf16[1,6,32,128]{3,2,1,0:T(8,128)(2,1)S(1)}, bf16[1,6,32,128]{3,2,1,0:T(8,128)(2,1)S(1)}, u32[]{:S(2)}, u32[]{:S(2)}) collective-permute-start(bf16[1,6,32,128]{3,2,1,0:T(8,128)(2,1)S(1)} %get-tuple-element.7), channel_id=1, source_target_pairs={{0,8},{1,9},{2,10},{3,11},{4,12},{5,13},{6,14},{7,15},{8,16},{9,17... | collective-permute-start | bytes 147464 | tf_op jit(solution)/shard_map/ppermute | solution.py:14
  104.8 10.9 %collective-permute-start.19 = (bf16[1,6,32,128]{3,2,1,0:T(8,128)(2,1)S(1)}, bf16[1,6,32,128]{3,2,1,0:T(8,128)(2,1)S(1)}, u32[]{:S(2)}, u32[]{:S(2)}) collective-permute-start(bf16[1,6,32,128]{3,2,1,0:T(8,128)(2,1)S(1)} %get-tuple-element.6), channel_id=1, source_target_pairs={{0,9},{1,10},{2,11},{3,12},{4,13},{5,14},{6,15},{7,16},{8,17},{9,1... | collective-permute-start | bytes 147464 | tf_op jit(solution)/shard_map/ppermute | solution.py:14
where the time goes:
time: 255 us; the launch traced here: 254 us
  blocking collectives  107 us (42%)
  starting transfers between devices  81.1 us (32%)
  other arithmetic  23.2 us (9%)
  local copies, waits for them, and re-layouts  16.1 us (6%)
  matrix products  15.3 us (6%)
  waiting for transfers between devices  8.56 us (3%)
    psum x1, blocking collectives, body(): gram_matrix = lax.psum(local_gram, ('group', 'dom'))  107 us
    ppermute x16, starting transfers between devices, from_behind(): lax.ppermute(value, axis, [(source, source + steps) for source in range(l...  68.1 us
    dot_general x2, matrix products, operate(): jnp.einsum('cfij,cfrj->cri', layer_weights[0], operands, preferred_elemen...  13 us
    ppermute x2, starting transfers between devices, extended(): before = lax.ppermute(last, axis, up)  10.5 us
    another operation x3, other arithmetic, body(): lower_factor = jnp.linalg.cholesky(gram_matrix)  9.45 us
    gather x1, local copies, waits for them, and re-layouts, body(): layer_weights = [templates[template_ids[0]]]  8.57 us
    ppermute x16, waiting for transfers between devices, from_behind(): lax.ppermute(value, axis, [(source, source + steps) for source in range(l...  8.55 us
    another operation x1, other arithmetic, body(): lax.linalg.triangular_solve(lower_factor, jnp.eye(basis_width, dtype=gram...  7.36 us
  transfers between devices with their start and end apart: 20, of which 3 were waited for; matrix products, arithmetic and copies ran while one was open for 8% of the time, Pallas kernels for 0%

commit v1 on v0

v1 whole, which is shorter than its diff:
```python
import functools
import math

import jax
import jax.numpy as jnp
from jax import lax
from jax.experimental import pallas as pl
from jax.experimental.pallas import tpu as pltpu
from jax.sharding import PartitionSpec as P

DIRECTIONS = ((-1, -1), (-1, 0), (-1, 1), (0, -1), (0, 1), (1, -1), (1, 0), (1, 1))
MESH = pl.DeviceIdType.MESH
F32 = jnp.float32
BF16 = jnp.bfloat16
NT = (((1,), (1,)), ((), ()))
HIGH = lax.Precision.HIGHEST


def dot(x, y):
    return jnp.dot(x, y, preferred_element_type=F32)


def dot_nt(x, y):
    return lax.dot_general(x, y, NT, preferred_element_type=F32)


def exact(x, y):
    return jnp.dot(x, y, preferred_element_type=F32, precision=HIGH)


def exact_nt(x, y):
    return lax.dot_general(x, y, NT, preferred_element_type=F32, precision=HIGH)


def kernel(
    groups, side, peers_y, rows_total,
    basis_ref, templates_ref, ids_ref, live_ref, refs_ref, lists_ref,
    q_ref, r_ref,
    tmpl, v0, v1, v2, ghost1, ghost2, packet1, packet2, layer1, layer2, acc,
    part, part_in, mid, mid_in, far, far_in, done, work, upper, inv,
    load_sem, halo_send, halo_recv, sum_send, sum_recv,
):
    column_cap, rhs, dof = v0.shape[0] - 1, v0.shape[1], v0.shape[2]
    halo_cap = packet1.shape[1]
    zero_own, zero_ghost = column_cap, 8 * halo_cap
    vectors, ghosts, layers = (v0, v1, v2), (ghost1, ghost2), (layer1, layer2)
    packets = (packet1, packet2)
    pieces = side * side
    peers_x = pieces // peers_y
    g = lax.axis_index("group")
    d = lax.axis_index("dom")
    row, col = d // side, d % side
    core, at_y, at_x = d % 2, (d // 2) % peers_y, d // (2 * peers_y)
    me_x = at_x * 2 + core

    def on_z(offset):
        return ((g + offset) % groups, d)

    def on_y(offset):
        return (g, (at_x * peers_y + (at_y + offset) % peers_y) * 2 + core)

    def on_x(offset):
        other = (me_x + offset) % peers_x
        return (g, ((other // 2) * peers_y + at_y) * 2 + other % 2)

    def inside(dx, dy):
        return (row + dx >= 0) & (row + dx < side) & (col + dy >= 0) & (col + dy < side)

    load_templates = pltpu.make_async_copy(templates_ref, tmpl, load_sem.at[0])
    load_templates.start()
    load_basis = pltpu.make_async_copy(basis_ref.at[0], v0.at[pl.ds(0, column_cap)], load_sem.at[1])
    load_basis.start()

    barrier = pltpu.get_barrier_semaphore()

    def greet(device):
        pl.semaphore_signal(barrier, inc=1, device_id=device, device_id_type=MESH)

    expected = 0
    for dx, dy in DIRECTIONS:
        target = (g, (row + dx) * side + col + dy)
        pl.when(inside(dx, dy))(functools.partial(greet, target))
        expected += inside(dx, dy).astype(jnp.int32)
    for peers, place in ((groups, on_z), (peers_y, on_y), (peers_x, on_x)):
        for offset in range(1, peers):
            greet(place(offset))
        expected += peers - 1

    empty = jnp.zeros((rhs, dof), BF16)
    for vector in vectors:
        vector[zero_own] = empty
    for x in range(2):
        ghosts[x][zero_ghost] = empty
        for k, (dx, dy) in enumerate(DIRECTIONS):
            @pl.when(jnp.logical_not(inside(-dx, -dy)))
            def _():
                ghosts[x][pl.ds(k * halo_cap, halo_cap)] = jnp.zeros((halo_cap, rhs, dof), BF16)

        @pl.when(g == 0)
        def _():
            layers[x][0] = jnp.zeros((column_cap, rhs, dof), BF16)

        @pl.when(g == groups - 1)
        def _():
            layers[x][1] = jnp.zeros((column_cap, rhs, dof), BF16)

    live = live_ref[0]
    load_basis.wait()

    @pl.loop(0, column_cap)
    def _(c):
        v0[c] = v0[c] * (c < live).astype(F32).astype(BF16)

    pl.semaphore_wait(barrier, expected)

    def plane_copy(x, k):
        dx, dy = DIRECTIONS[k]
        return pltpu.make_async_remote_copy(
            src_ref=packets[x].at[k],
            dst_ref=ghosts[x].at[pl.ds(k * halo_cap, halo_cap)],
            send_sem=halo_send.at[x, k],
            recv_sem=halo_recv.at[x, k],
            device_id=(g, (row + dx) * side + col + dy),
            device_id_type=MESH,
        )

    def layer_copy(x, up):
        return pltpu.make_async_remote_copy(
            src_ref=vectors[x].at[pl.ds(0, column_cap)],
            dst_ref=layers[x].at[0 if up else 1],
            send_sem=halo_send.at[x, 8 + up],
            recv_sem=halo_recv.at[x, 8 + up],
            device_id=(g + 1 if up else g - 1, d),
            device_id_type=MESH,
        )

    has_up, has_down = g < groups - 1, g > 0
    order = (6, 1, 5, 7, 0, 2, 3, 4)

    def halo_start(x):
        vector = vectors[x]
        for k in order:
            for s in range(halo_cap):
                slot = lists_ref[0, k, s]
                packets[x][k, s] = vector[jnp.where(slot < 0, zero_own, slot)]
            pl.when(inside(*DIRECTIONS[k]))(lambda: plane_copy(x, k).start())
        pl.when(has_up)(lambda: layer_copy(x, 1).start())
        pl.when(has_down)(lambda: layer_copy(x, 0).start())

    def layers_wait(x):
        pl.when(has_down)(lambda: layer_copy(x, 1).wait_recv())
        pl.when(has_up)(lambda: layer_copy(x, 0).wait_recv())

    def plane_wait(x):
        for k in order:
            dx, dy = DIRECTIONS[k]
            pl.when(inside(-dx, -dy))(lambda: plane_copy(x, k).wait_recv())

    def halo_sent(x):
        for k in order:
            pl.when(inside(*DIRECTIONS[k]))(lambda: plane_copy(x, k).wait_send())
        pl.when(has_up)(lambda: layer_copy(x, 1).wait_send())
        pl.when(has_down)(lambda: layer_copy(x, 0).wait_send())

    def apply(blocks, c, faces):
        weights = jnp.concatenate([tmpl[ids_ref[0, c, f]] for f in faces], axis=1)
        return dot_nt(jnp.concatenate(blocks, axis=1), weights)

    def own_pass(x):
        vector = vectors[x]

        @pl.loop(0, column_cap)
        def _(c):
            blocks = [vector[c]]
            for q in range(4):
                r = refs_ref[c, q]
                blocks.append(vector[jnp.where((r < 0) | (r >= column_cap), zero_own, r)])
            acc[c] = apply(blocks, c, (0, 3, 4, 5, 6))

    def layer_pass(x):
        @pl.loop(0, column_cap)
        def _(c):
            acc[c] = acc[c] + apply([layers[x][0, c], layers[x][1, c]], c, (1, 2))

    def ghost_pass(x):
        @pl.loop(0, column_cap)
        def _(c):
            blocks = []
            for q in range(4):
                r = refs_ref[c, q]
                blocks.append(ghosts[x][jnp.where(r < column_cap, zero_ghost, r - column_cap)])
            total = acc[c] + apply(blocks, c, (3, 4, 5, 6))
            vectors[x + 1][c] = jnp.where(c < live, total, 0.0).astype(BF16)

    def gram_rows(j):
        @functools.partial(lax.fori_loop, 0, column_cap // 2, init_val=jnp.zeros((rhs, rhs * (j + 1)), F32))
        def total(h, carry):
            pair = [
                jnp.concatenate([vectors[i][2 * h], vectors[i][2 * h + 1]], axis=1)
                for i in range(j + 1)
            ]
            return carry + dot_nt(pair[j], jnp.concatenate(pair, axis=0))

        work[:, : rhs * (j + 1)] = total

    share = rhs // groups

    def send_all(j, phase, peers, place, source, slots, at):
        copies = []
        for offset in range(1, peers):
            copies.append(pltpu.make_async_remote_copy(
                src_ref=source(offset),
                dst_ref=slots.at[j, at],
                send_sem=sum_send.at[j, phase, offset],
                recv_sem=sum_recv.at[j, phase, offset],
                device_id=place(offset),
                device_id_type=MESH,
            ))
        for copy in copies:
            copy.start()
        return copies

    def add_up(slots, j, peers):
        total = slots[j, 0]
        for s in range(1, peers):
            total = total + slots[j, s]
        return total

    def reduce_steps(j):
        for s in range(groups):
            part[j, s] = work[s * share : (s + 1) * share, :]
        part_in[j, g] = part[j, g]
        copies = send_all(j, 0, groups, on_z, lambda o: part.at[j, (g + o) % groups], part_in, g)
        yield
        for copy in copies:
            copy.wait()
        mid[j] = add_up(part_in, j, groups)
        mid_in[j, at_y] = mid[j]
        copies = send_all(j, 1, peers_y, on_y, lambda o: mid.at[j], mid_in, at_y)
        yield
        for copy in copies:
            copy.wait()
        far[j] = add_up(mid_in, j, peers_y)
        far_in[j, me_x] = far[j]
        copies = send_all(j, 2, peers_x, on_x, lambda o: far.at[j], far_in, me_x)
        yield
        for copy in copies:
            copy.wait()
        done[j, g] = add_up(far_in, j, peers_x)
        copies = send_all(j, 3, groups, on_z, lambda o: done.at[j, g], done, g)
        yield
        for copy in copies:
            copy.wait()
        for s in range(groups):
            work[s * share : (s + 1) * share, :] = done[j, s] * (1.0 / rows_total)
        yield

    lanes = work.shape[1]
    wide = lax.broadcasted_iota(jnp.int32, (rhs, lanes), 1)
    tall = lax.broadcasted_iota(jnp.int32, (rhs, lanes), 0)

    def factor(j):
        before = rhs * j
        corner = work[:, before : before + rhs]
        if j:
            left = exact_nt(work[:, :before], inv[:before, :before])
            corner = corner - exact_nt(left, left)
        work[...] = jnp.where(wide == tall + rhs, 1.0, 0.0)
        work[:, :rhs] = corner
        m = work[...]
        for p in range(rhs // 8):
            size = rhs - 8 * p
            cols = [jnp.broadcast_to(m[:, 8 * p + i : 8 * p + i + 1], (size, lanes)) for i in range(8)]
            for i in range(8):
                scale = lax.rsqrt(jnp.broadcast_to(cols[i][i : i + 1, :], (size, lanes)))
                column = cols[i] * scale
                line = jnp.broadcast_to(m[i : i + 1, :], (size, lanes)) * scale
                upper[8 * p + i : 8 * p + i + 1, :] = line[0:1, :]
                m = m - column * line
                for n in range(i + 1, 8):
                    cols[n] = cols[n] - column * jnp.broadcast_to(column[n : n + 1, :], (size, lanes))
            m = m[8:]
        square = lax.broadcasted_iota(jnp.int32, (rhs, rhs), 0)
        across = lax.broadcasted_iota(jnp.int32, (rhs, rhs), 1)
        r_ref[before : before + rhs, before : before + rhs] = jnp.where(
            across >= square, upper[:, :rhs], 0.0
        )
        corner_inv = upper[:, rhs : 2 * rhs]
        inv[before : before + rhs, before : before + rhs] = corner_inv
        if j:
            r_ref[:before, before : before + rhs] = left.T
            r_ref[before : before + rhs, :before] = jnp.zeros((rhs, before), F32)
            inv[before : before + rhs, :before] = -exact(corner_inv, exact(left, inv[:before, :before]))

    def project(j):
        width = rhs * (j + 1)
        rows = inv[rhs * j : width, :width]
        high = rows.astype(BF16)
        low = (rows - high.astype(F32)).astype(BF16)
        both = jnp.concatenate([high, low], axis=1)

        @pl.loop(0, column_cap)
        def _(c):
            stack = [vectors[i][c] for i in range(j + 1)]
            q_ref[0, c, rhs * j : width, :] = dot(both, jnp.concatenate(stack + stack, axis=0)).astype(BF16)

    halo_start(0)
    gram_rows(0)
    stage = reduce_steps(0)
    next(stage)
    load_templates.wait()
    own_pass(0)
    next(stage)
    layers_wait(0)
    layer_pass(0)
    next(stage)
    next(stage)
    plane_wait(0)
    ghost_pass(0)

    halo_start(1)
    next(stage)
    factor(0)
    project(0)
    gram_rows(1)
    stage = reduce_steps(1)
    next(stage)
    own_pass(1)
    next(stage)
    layers_wait(1)
    layer_pass(1)
    next(stage)
    next(stage)
    next(stage)
    factor(1)
    project(1)
    plane_wait(1)
    ghost_pass(1)

    gram_rows(2)
    for _ in reduce_steps(2):
        pass
    factor(2)
    project(2)
    halo_sent(0)
    halo_sent(1)


def solution(mesh):
    groups, pieces = mesh.shape["group"], mesh.shape["dom"]
    side = math.isqrt(pieces)
    peers_y = min(8, pieces // 2)
    peers_x = pieces // peers_y

    def body(basis_start, templates, template_ids, live_columns, face_refs, send_lists):
        _, column_cap, rhs, dof = basis_start.shape
        halo_cap = send_lists.shape[2]
        width = 3 * rhs
        share = rhs // groups
        lanes = 128
        rows_total = column_cap * dof * groups * pieces
        vmem, smem = pltpu.VMEM, pltpu.SMEM
        block = (rhs, dof)
        return pl.pallas_call(
            functools.partial(kernel, groups, side, peers_y, rows_total),
            out_shape=(
                jax.ShapeDtypeStruct((1, column_cap, width, dof), BF16),
                jax.ShapeDtypeStruct((width, width), F32),
            ),
            in_specs=[pl.BlockSpec(memory_space=pl.ANY)] * 2 + [pl.BlockSpec(memory_space=smem)] * 4,
            out_specs=(pl.BlockSpec(memory_space=vmem), pl.BlockSpec(memory_space=vmem)),
            scratch_shapes=[
                vmem(templates.shape, BF16),
                vmem((column_cap + 1, *block), BF16),
                vmem((column_cap + 1, *block), BF16),
                vmem((column_cap + 1, *block), BF16),
                vmem((8 * halo_cap + 1, *block), BF16),
                vmem((8 * halo_cap + 1, *block), BF16),
                vmem((8, halo_cap, *block), BF16),
                vmem((8, halo_cap, *block), BF16),
                vmem((2, column_cap, *block), BF16),
                vmem((2, column_cap, *block), BF16),
                vmem((column_cap, *block), F32),
                vmem((3, groups, share, lanes), F32),
                vmem((3, groups, share, lanes), F32),
                vmem((3, share, lanes), F32),
                vmem((3, peers_y, share, lanes), F32),
                vmem((3, share, lanes), F32),
                vmem((3, peers_x, share, lanes), F32),
                vmem((3, groups, share, lanes), F32),
                vmem((rhs, lanes), F32),
                vmem((rhs, lanes), F32),
                vmem((width, lanes), F32),
                pltpu.SemaphoreType.DMA((2,)),
                pltpu.SemaphoreType.DMA((2, 10)),
                pltpu.SemaphoreType.DMA((2, 10)),
                pltpu.SemaphoreType.DMA((3, 4, 8)),
                pltpu.SemaphoreType.DMA((3, 4, 8)),
            ],
            compiler_params=pltpu.CompilerParams(
                collective_id=0, has_side_effects=True, vmem_limit_bytes=40 * 2**20
            ),
        )(basis_start, templates, template_ids, live_columns, face_refs, send_lists)

    return jax.shard_map(
        body,
        mesh=mesh,
        in_specs=(
            P("group", "dom", None, None),
            P(),
            P("group", "dom", None),
            P("dom"),
            P("dom", None),
            P("dom", None, None),
        ),
        out_specs=(P("group", "dom", None, None), P()),
        check_vma=False,
    )
```

time: 255 us -> 119 us (0.47)
  Pallas kernels: 0 us -> 111 us
  blocking collectives: 107 us -> 0 us
  starting transfers between devices: 81.1 us -> 0 us
  other arithmetic: 23.2 us -> 0 us
  matrix products: 15.3 us -> 0 us
  local copies, waits for them, and re-layouts: 16.1 us -> 6.4 us
  waiting for transfers between devices: 8.56 us -> 0 us
    pallas_call x0 -> x1, Pallas kernels: none -> 111 us  [body(): pl.pallas_call(functools.partial(kernel, groups, side, peers_y, rows_tota...]
    psum x1 -> x0, blocking collectives: 107 us -> none  [body(): gram_matrix = lax.psum(local_gram, ('group', 'dom'))]
    ppermute x20 -> x0, starting transfers between devices: 81.1 us -> none  [the longest x16 68.1 us: from_behind(): lax.ppermute(value, axis, [(source, source + steps) for source in range(l...]
    another operation x5 -> x0, other arithmetic: 16.9 us -> none  [the longest x3 9.45 us: body(): lower_factor = jnp.linalg.cholesky(gram_matrix)]
    dot_general x5 -> x0, matrix products: 15.1 us -> none  [the longest x2 13 us: operate(): jnp.einsum('cfij,cfrj->cri', layer_weights[0], operands, preferred_elemen...]
    gather x5 -> x0, local copies, waits for them, and re-layouts: 13.7 us -> none  [the longest x1 8.57 us: body(): layer_weights = [templates[template_ids[0]]]]
    ppermute x20 -> x0, waiting for transfers between devices: 8.56 us -> none  [the longest x16 8.55 us: from_behind(): lax.ppermute(value, axis, [(source, source + steps) for source in range(l...]
    select_n x8 -> x0, other arithmetic: 5.43 us -> none  [the longest x2 2.98 us: operate(): jnp.where(valid_ref[None, :, :, None, None], beside, jnp.zeros((), jnp.bf...]
  transfers between devices with their start and end apart: 20 -> 0, of which waited for: 3 -> 0; matrix products, arithmetic and copies ran while one was open for 8% -> 0% of each run, Pallas kernels for 0% -> 0%
where the time goes in v1:
time: 119 us
  Pallas kernels  111 us (93%)
  local copies, waits for them, and re-layouts  6.4 us (5%)
  between operations  1.29 us (1%)
    pallas_call x1, Pallas kernels, body(): pl.pallas_call(functools.partial(kernel, groups, side, peers_y, rows_tota...  111 us
    unnamed x9, local copies, waits for them, and re-layouts  6.4 us

profile of v1, /device:TPU:1, one launch (start us, length us, event | category | flops | bytes accessed | tf_op | source)
XLA Modules:
  0.0 118.6 jit_solution(7542457176476716385)
XLA Ops:
  1.3 0.8 copy.10.lists_ref
  2.0 0.8 copy.8.ids_ref
  2.8 0.8 copy.9.refs_ref
  3.6 0.0 copy-start
  3.6 1.6 %copy-done = bf16[64,128,128]{2,1,0:T(8,128)(2,1)S(1)} copy-done((bf16[64,128,128]{2,1,0:T(8,128)(2,1)S(1)}, bf16[64,128,128]{2,1,0:T(8,128)(2,1)}, u32[]{:S(2)}) %copy-start) | copy-done | bytes 2097176
  5.2 0.0 copy-start.1
  5.2 1.0 copy-done.1
  6.1 111.0 %shard_map.77 = (bf16[1,36,96,128]{3,2,1,0:T(8,128)(2,1)S(1)}, f32[96,96]{1,0:T(8,128)S(1)}) custom-call(bf16[1,36,32,128]{3,2,1,0:T(8,128)(2,1)S(1)} %copy-done.1, bf16[64,128,128]{2,1,0:T(8,128)(2,1)S(1)} %copy-done, s32[1,36,7]{2,1,0:T(8,128)S(1)} %copy.8.ids_ref, s32[1]{0:T(128)S(6)} %copy.13.live_ref, s32[36,4]{1,0:T(8,128)S(1)} %copy.9.refs_ref, ...), custom_call_target="tpu_custom_call" | custom-call | tf_op jit(solution)/shard_map/pallas_call | solution.py:364
  117.1 0.9 copy.14
  118.0 0.6 copy.15
Async XLA Ops:
  3.6 1.6 %copy-start = (bf16[64,128,128]{2,1,0:T(8,128)(2,1)S(1)}, bf16[64,128,128]{2,1,0:T(8,128)(2,1)}, u32[]{:S(2)}) copy-start(bf16[64,128,128]{2,1,0:T(8,128)(2,1)} %templates_ref.1) | copy-start | bytes 6291460
  5.2 1.0 copy-start.1

commit v2 on v1

--- a/solution.py
+++ b/solution.py
@@ -14,6 +14,8 @@
 BF16 = jnp.bfloat16
 NT = (((1,), (1,)), ((), ()))
 HIGH = lax.Precision.HIGHEST
+UN_OWN = UN_LAYER = UN_GHOST = UN_PROJ = 12
+UN_GRAM = 9
 
 
 def dot(x, y):
@@ -37,7 +39,7 @@
     basis_ref, templates_ref, ids_ref, live_ref, refs_ref, lists_ref,
     q_ref, r_ref,
     tmpl, v0, v1, v2, ghost1, ghost2, packet1, packet2, layer1, layer2, acc,
-    part, part_in, mid, mid_in, far, far_in, done, work, upper, inv,
+    slots_a, slots_b, work, upper, inv,
     load_sem, halo_send, halo_recv, sum_send, sum_recv,
 ):
     column_cap, rhs, dof = v0.shape[0] - 1, v0.shape[1], v0.shape[2]
@@ -104,6 +106,7 @@
         def _():
             layers[x][1] = jnp.zeros((column_cap, rhs, dof), BF16)
 
+    inv[...] = jnp.zeros(inv.shape, F32)
     live = live_ref[0]
     load_basis.wait()
 
@@ -140,12 +143,13 @@
     def halo_start(x):
         vector = vectors[x]
         for k in order:
+            if k == 3:
+                pl.when(has_up)(lambda: layer_copy(x, 1).start())
+                pl.when(has_down)(lambda: layer_copy(x, 0).start())
             for s in range(halo_cap):
-                slot = lists_ref[0, k, s]
+                slot = lists_ref[s, 0, k]
                 packets[x][k, s] = vector[jnp.where(slot < 0, zero_own, slot)]
             pl.when(inside(*DIRECTIONS[k]))(lambda: plane_copy(x, k).start())
-        pl.when(has_up)(lambda: layer_copy(x, 1).start())
-        pl.when(has_down)(lambda: layer_copy(x, 0).start())
 
     def layers_wait(x):
         pl.when(has_down)(lambda: layer_copy(x, 1).wait_recv())
@@ -163,107 +167,114 @@
         pl.when(has_down)(lambda: layer_copy(x, 0).wait_send())
 
     def apply(blocks, c, faces):
-        weights = jnp.concatenate([tmpl[ids_ref[0, c, f]] for f in faces], axis=1)
-        return dot_nt(jnp.concatenate(blocks, axis=1), weights)
+        weights = jnp.concatenate([tmpl[ids_ref[f, 0, c]] for f in faces], axis=0)
+        return dot(jnp.concatenate(blocks, axis=1), weights)
 
     def own_pass(x):
         vector = vectors[x]
 
-        @pl.loop(0, column_cap)
+        @pl.loop(0, column_cap, unroll=UN_OWN)
         def _(c):
             blocks = [vector[c]]
             for q in range(4):
-                r = refs_ref[c, q]
+                r = refs_ref[q, c]
                 blocks.append(vector[jnp.where((r < 0) | (r >= column_cap), zero_own, r)])
             acc[c] = apply(blocks, c, (0, 3, 4, 5, 6))
 
     def layer_pass(x):
-        @pl.loop(0, column_cap)
+        @pl.loop(0, column_cap, unroll=UN_LAYER)
         def _(c):
             acc[c] = acc[c] + apply([layers[x][0, c], layers[x][1, c]], c, (1, 2))
 
     def ghost_pass(x):
-        @pl.loop(0, column_cap)
+        @pl.loop(0, column_cap, unroll=UN_GHOST)
         def _(c):
             blocks = []
             for q in range(4):
-                r = refs_ref[c, q]
+                r = refs_ref[q, c]
                 blocks.append(ghosts[x][jnp.where(r < column_cap, zero_ghost, r - column_cap)])
             total = acc[c] + apply(blocks, c, (3, 4, 5, 6))
             vectors[x + 1][c] = jnp.where(c < live, total, 0.0).astype(BF16)
 
-    def gram_rows(j):
-        @functools.partial(lax.fori_loop, 0, column_cap // 2, init_val=jnp.zeros((rhs, rhs * (j + 1)), F32))
-        def total(h, carry):
+    def gram(rows):
+        def add(h, carry):
             pair = [
                 jnp.concatenate([vectors[i][2 * h], vectors[i][2 * h + 1]], axis=1)
-                for i in range(j + 1)
+                for i in range(rows[-1] + 1)
             ]
-            return carry + dot_nt(pair[j], jnp.concatenate(pair, axis=0))
-
-        work[:, : rhs * (j + 1)] = total
-
-    share = rhs // groups
-
-    def send_all(j, phase, peers, place, source, slots, at):
-        copies = []
-        for offset in range(1, peers):
-            copies.append(pltpu.make_async_remote_copy(
-                src_ref=source(offset),
-                dst_ref=slots.at[j, at],
-                send_sem=sum_send.at[j, phase, offset],
-                recv_sem=sum_recv.at[j, phase, offset],
+            return tuple(
+                total + dot_nt(pair[j], jnp.concatenate(pair[: j + 1], axis=0))
+                for j, total in zip(rows, carry)
+            )
+
+        start = tuple(jnp.zeros((rhs, rhs * (j + 1)), F32) for j in rows)
+        totals = lax.fori_loop(0, column_cap // 2, add, start, unroll=UN_GRAM)
+        return [t[:, rhs * i : rhs * (i + 1)] for t in totals for i in range(t.shape[1] // rhs)]
+
+    def pack(block):
+        return jnp.concatenate([block[8 * i : 8 * i + 8] for i in range(rhs // 8)], axis=1)
+
+    def unpack(line):
+        return jnp.concatenate([line[:, rhs * i : rhs * (i + 1)] for i in range(rhs // 8)], axis=0)
+
+    def send_all(w, hop, peers, place, source, slots, at):
+        copies = [
+            pltpu.make_async_remote_copy(
+                src_ref=source,
+                dst_ref=slots.at[at],
+                send_sem=sum_send.at[w, hop, offset],
+                recv_sem=sum_recv.at[w, hop, offset],
                 device_id=place(offset),
                 device_id_type=MESH,
-            ))
+            )
+            for offset in range(1, peers)
+        ]
         for copy in copies:
             copy.start()
         return copies
 
-    def add_up(slots, j, peers):
-        total = slots[j, 0]
+    def add_up(slots, peers):
+        total = slots[0]
         for s in range(1, peers):
-            total = total + slots[j, s]
+            total = total + slots[s]
         return total
 
-    def reduce_steps(j):
-        for s in range(groups):
-            part[j, s] = work[s * share : (s + 1) * share, :]
-        part_in[j, g] = part[j, g]
-        copies = send_all(j, 0, groups, on_z, lambda o: part.at[j, (g + o) % groups], part_in, g)
-        yield
-        for copy in copies:
-            copy.wait()
-        mid[j] = add_up(part_in, j, groups)
-        mid_in[j, at_y] = mid[j]
-        copies = send_all(j, 1, peers_y, on_y, lambda o: mid.at[j], mid_in, at_y)
-        yield
-        for copy in copies:
-            copy.wait()
-        far[j] = add_up(mid_in, j, peers_y)
-        far_in[j, me_x] = far[j]
-        copies = send_all(j, 2, peers_x, on_x, lambda o: far.at[j], far_in, me_x)
-        yield
-        for copy in copies:
-            copy.wait()
-        done[j, g] = add_up(far_in, j, peers_x)
-        copies = send_all(j, 3, groups, on_z, lambda o: done.at[j, g], done, g)
-        yield
-        for copy in copies:
-            copy.wait()
-        for s in range(groups):
-            work[s * share : (s + 1) * share, :] = done[j, s] * (1.0 / rows_total)
-        yield
+    axes_z, axes_y, axes_x = (groups, on_z, g), (peers_y, on_y, at_y), (peers_x, on_x, me_x)
+
+    def reduced(w, blocks):
+        routes = ((axes_y, axes_z, axes_x), (axes_z, axes_y, axes_x))
+        sums = [
+            jnp.concatenate([pack(blocks[0]), pack(blocks[1])], axis=0),
+            pack(blocks[2]),
+        ]
+        sent = []
+        for hop in range(3):
+            pending = []
+            for way, total in enumerate(sums):
+                peers, place, at = routes[way][hop]
+                slots = (slots_a, slots_b)[way].at[w, hop]
+                slots[at] = total
+                copies = send_all(2 * w + way, hop, peers, place, slots.at[at], slots, at)
+                pending.append((slots, peers, copies))
+            yield None
+            sums = []
+            for slots, peers, copies in pending:
+                for copy in copies:
+                    copy.wait_recv()
+                sent += copies
+                sums.append(add_up(slots, peers))
+        whole = [sums[0][:8], sums[0][8:], sums[1]]
+        yield [unpack(line) * (1.0 / rows_total) for line in whole], sent
 
     lanes = work.shape[1]
     wide = lax.broadcasted_iota(jnp.int32, (rhs, lanes), 1)
     tall = lax.broadcasted_iota(jnp.int32, (rhs, lanes), 0)
 
-    def factor(j):
+    def factor(j, blocks):
         before = rhs * j
-        corner = work[:, before : before + rhs]
+        corner = blocks[j]
         if j:
-            left = exact_nt(work[:, :before], inv[:before, :before])
+            left = exact_nt(jnp.concatenate(blocks[:j], axis=1), inv[:before, :before])
             corner = corner - exact_nt(left, left)
         work[...] = jnp.where(wide == tall + rhs, 1.0, 0.0)
         work[:, :rhs] = corner
@@ -299,51 +310,51 @@
         low = (rows - high.astype(F32)).astype(BF16)
         both = jnp.concatenate([high, low], axis=1)
 
-        @pl.loop(0, column_cap)
+        @pl.loop(0, column_cap, unroll=UN_PROJ)
         def _(c):
             stack = [vectors[i][c] for i in range(j + 1)]
             q_ref[0, c, rhs * j : width, :] = dot(both, jnp.concatenate(stack + stack, axis=0)).astype(BF16)
 
     halo_start(0)
-    gram_rows(0)
-    stage = reduce_steps(0)
-    next(stage)
     load_templates.wait()
+
+    @pl.loop(0, tmpl.shape[0], unroll=4)
+    def _(t):
+        tmpl[t] = tmpl[t].T
+
     own_pass(0)
-    next(stage)
     layers_wait(0)
     layer_pass(0)
-    next(stage)
-    next(stage)
     plane_wait(0)
     ghost_pass(0)
 
     halo_start(1)
-    next(stage)
-    factor(0)
-    project(0)
-    gram_rows(1)
-    stage = reduce_steps(1)
-    next(stage)
+    early = reduced(0, gram((0, 1)))
+    next(early)
     own_pass(1)
-    next(stage)
     layers_wait(1)
     layer_pass(1)
-    next(stage)
-    next(stage)
-    next(stage)
-    factor(1)
-    project(1)
+    next(early)
     plane_wait(1)
     ghost_pass(1)
 
-    gram_rows(2)
-    for _ in reduce_steps(2):
-        pass
-    factor(2)
+    late = reduced(1, gram((2,)))
+    next(late)
+    next(early)
+    next(late)
+    (first, *second), sent_early = next(early)
+    factor(0, [first])
+    project(0)
+    factor(1, second)
+    next(late)
+    project(1)
+    third, sent_late = next(late)
+    factor(2, third)
     project(2)
     halo_sent(0)
     halo_sent(1)
+    for copy in sent_early + sent_late:
+        copy.wait_send()
 
 
 def solution(mesh):
@@ -356,7 +367,6 @@
         _, column_cap, rhs, dof = basis_start.shape
         halo_cap = send_lists.shape[2]
         width = 3 * rhs
-        share = rhs // groups
         lanes = 128
         rows_total = column_cap * dof * groups * pieces
         vmem, smem = pltpu.VMEM, pltpu.SMEM
@@ -367,7 +377,7 @@
                 jax.ShapeDtypeStruct((1, column_cap, width, dof), BF16),
                 jax.ShapeDtypeStruct((width, width), F32),
             ),
-            in_specs=[pl.BlockSpec(memory_space=pl.ANY)] * 2 + [pl.BlockSpec(memory_space=smem)] * 4,
+            in_specs=[pl.BlockSpec(memory_space=pltpu.HBM)] * 2 + [pl.BlockSpec(memory_space=smem)] * 4,
             out_specs=(pl.BlockSpec(memory_space=vmem), pl.BlockSpec(memory_space=vmem)),
             scratch_shapes=[
                 vmem(templates.shape, BF16),
@@ -381,26 +391,28 @@
                 vmem((2, column_cap, *block), BF16),
                 vmem((2, column_cap, *block), BF16),
                 vmem((column_cap, *block), F32),
-                vmem((3, groups, share, lanes), F32),
-                vmem((3, groups, share, lanes), F32),
-                vmem((3, share, lanes), F32),
-                vmem((3, peers_y, share, lanes), F32),
-                vmem((3, share, lanes), F32),
-                vmem((3, peers_x, share, lanes), F32),
-                vmem((3, groups, share, lanes), F32),
+                vmem((2, 3, 8, 16, lanes), F32),
+                vmem((2, 3, 8, 8, lanes), F32),
                 vmem((rhs, lanes), F32),
                 vmem((rhs, lanes), F32),
                 vmem((width, lanes), F32),
                 pltpu.SemaphoreType.DMA((2,)),
                 pltpu.SemaphoreType.DMA((2, 10)),
                 pltpu.SemaphoreType.DMA((2, 10)),
-                pltpu.SemaphoreType.DMA((3, 4, 8)),
-                pltpu.SemaphoreType.DMA((3, 4, 8)),
+                pltpu.SemaphoreType.DMA((4, 3, 8)),
+                pltpu.SemaphoreType.DMA((4, 3, 8)),
             ],
             compiler_params=pltpu.CompilerParams(
                 collective_id=0, has_side_effects=True, vmem_limit_bytes=40 * 2**20
             ),
-        )(basis_start, templates, template_ids, live_columns, face_refs, send_lists)
+        )(
+            basis_start,
+            templates,
+            template_ids.transpose(2, 0, 1),
+            live_columns,
+            face_refs.T,
+            send_lists.transpose(2, 0, 1),
+        )
 
     return jax.shard_map(
         body,

time: 119 us -> 80.6 us (0.68)
  Pallas kernels: 111 us -> 72.9 us
    pallas_call x1, Pallas kernels: 111 us -> 72.9 us  [body(): pl.pallas_call(functools.partial(kernel, groups, side, peers_y, rows_tota...]
    unnamed x9 -> x12, local copies, waits for them, and re-layouts: 6.4 us -> 6.13 us
where the time goes in v2:
time: 80.6 us; the launch traced here: 80.4 us
  Pallas kernels  72.9 us (90%)
  local copies, waits for them, and re-layouts  6.13 us (8%)
  between operations  1.3 us (2%)
    pallas_call x1, Pallas kernels, body(): pl.pallas_call(functools.partial(kernel, groups, side, peers_y, rows_tota...  72.9 us
    unnamed x12, local copies, waits for them, and re-layouts  6.13 us

profile of v2, /device:TPU:1, one launch (start us, length us, event | category | flops | bytes accessed | tf_op | source)
XLA Modules:
  0.0 80.4 jit_solution(2329778653553286912)
XLA Ops:
  1.3 0.0 copy-start
  1.3 1.6 %copy-done = bf16[64,128,128]{2,1,0:T(8,128)(2,1)S(1)} copy-done((bf16[64,128,128]{2,1,0:T(8,128)(2,1)S(1)}, bf16[64,128,128]{2,1,0:T(8,128)(2,1)}, u32[]{:S(2)}) %copy-start) | copy-done | bytes 2097176
  2.9 0.0 copy-start.1
  2.9 1.0 %copy-done.1 = bf16[1,36,32,128]{3,2,1,0:T(8,128)(2,1)S(1)} copy-done((bf16[1,36,32,128]{3,2,1,0:T(8,128)(2,1)S(1)}, bf16[1,36,32,128]{3,2,1,0:T(8,128)(2,1)}, u32[]{:S(2)}) %copy-start.1) | copy-done | bytes 294936
  3.8 0.0 copy-start.2
  3.8 0.7 copy-done.2
  4.5 0.0 copy-start.3
  4.5 0.7 copy-done.3
  5.2 0.0 copy-start.4
  5.2 0.7 copy-done.4
  5.9 72.9 %shard_map.77 = (bf16[1,36,96,128]{3,2,1,0:T(8,128)(2,1)S(1)}, f32[96,96]{1,0:T(8,128)S(1)}) custom-call(bf16[1,36,32,128]{3,2,1,0:T(8,128)(2,1)S(1)} %copy-done.1, bf16[64,128,128]{2,1,0:T(8,128)(2,1)S(1)} %copy-done, s32[7,1,36]{2,1,0:T(1,128)S(1)} %bitcast.3, s32[1]{0:T(128)S(6)} %copy.10.live_ref, s32[4,36]{1,0:T(4,128)S(1)} %bitcast.5, ...), custom_call_target="tpu_custom_call" | custom-call | tf_op jit(solution)/shard_map/pallas_call | solution.py:374
  78.8 0.9 %copy.11 = bf16[1,36,96,128]{3,2,1,0:T(8,128)(2,1)} copy(bf16[1,36,96,128]{3,2,1,0:T(8,128)(2,1)S(1)} %get-tuple-element.4) | data formatting | bytes 1769472
  79.8 0.6 copy.12
Async XLA Ops:
  1.3 1.6 %copy-start = (bf16[64,128,128]{2,1,0:T(8,128)(2,1)S(1)}, bf16[64,128,128]{2,1,0:T(8,128)(2,1)}, u32[]{:S(2)}) copy-start(bf16[64,128,128]{2,1,0:T(8,128)(2,1)} %templates_ref.1) | copy-start | bytes 6291460
  2.9 1.0 %copy-start.1 = (bf16[1,36,32,128]{3,2,1,0:T(8,128)(2,1)S(1)}, bf16[1,36,32,128]{3,2,1,0:T(8,128)(2,1)}, u32[]{:S(2)}) copy-start(bf16[1,36,32,128]{3,2,1,0:T(8,128)(2,1)} %basis_ref.1) | copy-start | bytes 884740
  3.8 0.7 copy-start.2
  4.5 0.7 copy-start.3
  5.2 0.7 copy-start.4

commit v3 on v2

--- a/solution.py
+++ b/solution.py
@@ -14,8 +14,9 @@
 BF16 = jnp.bfloat16
 NT = (((1,), (1,)), ((), ()))
 HIGH = lax.Precision.HIGHEST
-UN_OWN = UN_LAYER = UN_GHOST = UN_PROJ = 12
-UN_GRAM = 9
+VMEM_MIB = 60
+UN_OWN = UN_LAYER = UN_GHOST = UN_PROJ = 36
+UN_GRAM = 18
 
 
 def dot(x, y):
@@ -36,9 +37,9 @@
 
 def kernel(
     groups, side, peers_y, rows_total,
-    basis_ref, templates_ref, ids_ref, live_ref, refs_ref, lists_ref,
+    basis_ref, templates_ref, ids_in, live_in, refs_in, lists_in,
     q_ref, r_ref,
-    tmpl, v0, v1, v2, ghost1, ghost2, packet1, packet2, layer1, layer2, acc,
+    ids_ref, live_ref, refs_ref, lists_ref, tmpl, v0, v1, v2, ghost1, ghost2, packet1, packet2, layer1, layer2, acc,
     slots_a, slots_b, work, upper, inv,
     load_sem, halo_send, halo_recv, sum_send, sum_recv,
 ):
@@ -68,6 +69,14 @@
     def inside(dx, dy):
         return (row + dx >= 0) & (row + dx < side) & (col + dy >= 0) & (col + dy < side)
 
+    loads = [
+        pltpu.make_async_copy(source, target, load_sem.at[2 + i])
+        for i, (source, target) in enumerate(
+            ((lists_in, lists_ref), (live_in, live_ref), (ids_in, ids_ref), (refs_in, refs_ref))
+        )
+    ]
+    for load in loads:
+        load.start()
     load_templates = pltpu.make_async_copy(templates_ref, tmpl, load_sem.at[0])
     load_templates.start()
     load_basis = pltpu.make_async_copy(basis_ref.at[0], v0.at[pl.ds(0, column_cap)], load_sem.at[1])
@@ -107,6 +116,8 @@
             layers[x][1] = jnp.zeros((column_cap, rhs, dof), BF16)
 
     inv[...] = jnp.zeros(inv.shape, F32)
+    for load in loads:
+        load.wait()
     live = live_ref[0]
     load_basis.wait()
 
@@ -366,6 +377,7 @@
     def body(basis_start, templates, template_ids, live_columns, face_refs, send_lists):
         _, column_cap, rhs, dof = basis_start.shape
         halo_cap = send_lists.shape[2]
+        faces = template_ids.shape[2]
         width = 3 * rhs
         lanes = 128
         rows_total = column_cap * dof * groups * pieces
@@ -377,9 +389,13 @@
                 jax.ShapeDtypeStruct((1, column_cap, width, dof), BF16),
                 jax.ShapeDtypeStruct((width, width), F32),
             ),
-            in_specs=[pl.BlockSpec(memory_space=pltpu.HBM)] * 2 + [pl.BlockSpec(memory_space=smem)] * 4,
+            in_specs=[pl.BlockSpec(memory_space=pltpu.HBM)] * 6,
             out_specs=(pl.BlockSpec(memory_space=vmem), pl.BlockSpec(memory_space=vmem)),
             scratch_shapes=[
+                smem((faces, 1, column_cap), jnp.int32),
+                smem((1,), jnp.int32),
+                smem((4, column_cap), jnp.int32),
+                smem((halo_cap, 1, 8), jnp.int32),
                 vmem(templates.shape, BF16),
                 vmem((column_cap + 1, *block), BF16),
                 vmem((column_cap + 1, *block), BF16),
@@ -396,14 +412,14 @@
                 vmem((rhs, lanes), F32),
                 vmem((rhs, lanes), F32),
                 vmem((width, lanes), F32),
-                pltpu.SemaphoreType.DMA((2,)),
+                pltpu.SemaphoreType.DMA((6,)),
                 pltpu.SemaphoreType.DMA((2, 10)),
                 pltpu.SemaphoreType.DMA((2, 10)),
                 pltpu.SemaphoreType.DMA((4, 3, 8)),
                 pltpu.SemaphoreType.DMA((4, 3, 8)),
             ],
             compiler_params=pltpu.CompilerParams(
-                collective_id=0, has_side_effects=True, vmem_limit_bytes=40 * 2**20
+                collective_id=0, has_side_effects=True, vmem_limit_bytes=VMEM_MIB * 2**20
             ),
         )(
             basis_start,

time: 80.6 us -> 77.6 us (0.963)
  local copies, waits for them, and re-layouts: 6.13 us -> 3.56 us
    unnamed x12 -> x2, local copies, waits for them, and re-layouts: 6.13 us -> 3.56 us
where the time goes in v3:
time: 77.6 us; the launch traced here: 77.3 us
  Pallas kernels  72.5 us (93%)
  local copies, waits for them, and re-layouts  3.56 us (5%)
  between operations  1.29 us (2%)
    pallas_call x1, Pallas kernels, body(): pl.pallas_call(functools.partial(kernel, groups, side, peers_y, rows_tota...  72.5 us
    unnamed x2, local copies, waits for them, and re-layouts  3.56 us

profile of v3, /device:TPU:1, one launch (start us, length us, event | category | flops | bytes accessed | tf_op | source)
XLA Modules:
  0.0 77.3 jit_solution(9121930637251908358)
XLA Ops:
  1.3 72.5 %shard_map.77 = (bf16[1,36,96,128]{3,2,1,0:T(8,128)(2,1)}, f32[96,96]{1,0:T(8,128)}) custom-call(bf16[1,36,32,128]{3,2,1,0:T(8,128)(2,1)} %basis_ref.1, bf16[64,128,128]{2,1,0:T(8,128)(2,1)} %templates_ref.1, s32[7,1,36]{2,1,0:T(1,128)} %bitcast.3, s32[1]{0:T(128)S(6)} %copy.10.live_in, s32[4,36]{1,0:T(4,128)} %bitcast.5, s32[6,1,8]{2,1,0:T(1,128)} %bitcast.4), custom_call_target="tpu_custom_call" | custom-call | tf_op jit(solution)/shard_map/pallas_call | solution.py:386
  73.8 2.1 %copy.11 = bf16[1,36,96,128]{3,2,1,0:T(8,128)(2,1)} copy(bf16[1,36,96,128]{3,2,1,0:T(8,128)(2,1)} %get-tuple-element.4) | data formatting | bytes 1769472
  75.9 1.4 %copy.12 = f32[96,96]{1,0:T(8,128)} copy(f32[96,96]{1,0:T(8,128)} %get-tuple-element.5) | data formatting | bytes 73728

commit v4 on v3

--- a/solution.py
+++ b/solution.py
@@ -9,12 +9,13 @@
 from jax.sharding import PartitionSpec as P
 
 DIRECTIONS = ((-1, -1), (-1, 0), (-1, 1), (0, -1), (0, 1), (1, -1), (1, 0), (1, 1))
+ORDER = (6, 1, 5, 7, 0, 2, 3, 4)
 MESH = pl.DeviceIdType.MESH
 F32 = jnp.float32
 BF16 = jnp.bfloat16
 NT = (((1,), (1,)), ((), ()))
 HIGH = lax.Precision.HIGHEST
-VMEM_MIB = 60
+VMEM_MIB = 58
 UN_OWN = UN_LAYER = UN_GHOST = UN_PROJ = 36
 UN_GRAM = 18
 
@@ -69,6 +70,21 @@
     def inside(dx, dy):
         return (row + dx >= 0) & (row + dx < side) & (col + dy >= 0) & (col + dy < side)
 
+    barrier = pltpu.get_barrier_semaphore()
+
+    def greet(device):
+        pl.semaphore_signal(barrier, inc=1, device_id=device, device_id_type=MESH)
+
+    expected = 0
+    for dx, dy in (DIRECTIONS[k] for k in ORDER):
+        target = (g, (row + dx) * side + col + dy)
+        pl.when(inside(dx, dy))(functools.partial(greet, target))
+        expected += inside(dx, dy).astype(jnp.int32)
+    for peers, place in ((groups, on_z), (peers_y, on_y), (peers_x, on_x)):
+        for offset in range(1, peers):
+            greet(place(offset))
+        expected += peers - 1
+
     loads = [
         pltpu.make_async_copy(source, target, load_sem.at[2 + i])
         for i, (source, target) in enumerate(
@@ -82,21 +98,6 @@
     load_basis = pltpu.make_async_copy(basis_ref.at[0], v0.at[pl.ds(0, column_cap)], load_sem.at[1])
     load_basis.start()
 
-    barrier = pltpu.get_barrier_semaphore()
-
-    def greet(device):
-        pl.semaphore_signal(barrier, inc=1, device_id=device, device_id_type=MESH)
-
-    expected = 0
-    for dx, dy in DIRECTIONS:
-        target = (g, (row + dx) * side + col + dy)
-        pl.when(inside(dx, dy))(functools.partial(greet, target))
-        expected += inside(dx, dy).astype(jnp.int32)
-    for peers, place in ((groups, on_z), (peers_y, on_y), (peers_x, on_x)):
-        for offset in range(1, peers):
-            greet(place(offset))
-        expected += peers - 1
-
     empty = jnp.zeros((rhs, dof), BF16)
     for vector in vectors:
         vector[zero_own] = empty
@@ -124,8 +125,6 @@
     @pl.loop(0, column_cap)
     def _(c):
         v0[c] = v0[c] * (c < live).astype(F32).astype(BF16)
-
-    pl.semaphore_wait(barrier, expected)
 
     def plane_copy(x, k):
         dx, dy = DIRECTIONS[k]
@@ -149,17 +148,19 @@
         )
 
     has_up, has_down = g < groups - 1, g > 0
-    order = (6, 1, 5, 7, 0, 2, 3, 4)
-
-    def halo_start(x):
-        vector = vectors[x]
-        for k in order:
+
+    def pack_packet(x, k):
+        for s in range(halo_cap):
+            slot = lists_ref[s, 0, k]
+            packets[x][k, s] = vectors[x][jnp.where(slot < 0, zero_own, slot)]
+
+    def halo_start(x, packed):
+        for k in ORDER:
             if k == 3:
                 pl.when(has_up)(lambda: layer_copy(x, 1).start())
                 pl.when(has_down)(lambda: layer_copy(x, 0).start())
-            for s in range(halo_cap):
-                slot = lists_ref[s, 0, k]
-                packets[x][k, s] = vector[jnp.where(slot < 0, zero_own, slot)]
+            if not packed:
+                pack_packet(x, k)
             pl.when(inside(*DIRECTIONS[k]))(lambda: plane_copy(x, k).start())
 
     def layers_wait(x):
@@ -167,12 +168,12 @@
         pl.when(has_up)(lambda: layer_copy(x, 0).wait_recv())
 
     def plane_wait(x):
-        for k in order:
+        for k in ORDER:
             dx, dy = DIRECTIONS[k]
             pl.when(inside(-dx, -dy))(lambda: plane_copy(x, k).wait_recv())
 
     def halo_sent(x):
-        for k in order:
+        for k in ORDER:
             pl.when(inside(*DIRECTIONS[k]))(lambda: plane_copy(x, k).wait_send())
         pl.when(has_up)(lambda: layer_copy(x, 1).wait_send())
         pl.when(has_down)(lambda: layer_copy(x, 0).wait_send())
@@ -287,6 +288,7 @@
         if j:
             left = exact_nt(jnp.concatenate(blocks[:j], axis=1), inv[:before, :before])
             corner = corner - exact_nt(left, left)
+            across_inv = exact(left, inv[:before, :before])
         work[...] = jnp.where(wide == tall + rhs, 1.0, 0.0)
         work[:, :rhs] = corner
         m = work[...]
@@ -312,7 +314,7 @@
         if j:
             r_ref[:before, before : before + rhs] = left.T
             r_ref[before : before + rhs, :before] = jnp.zeros((rhs, before), F32)
-            inv[before : before + rhs, :before] = -exact(corner_inv, exact(left, inv[:before, :before]))
+            inv[before : before + rhs, :before] = -exact(corner_inv, across_inv)
 
     def project(j):
         width = rhs * (j + 1)
@@ -326,7 +328,10 @@
             stack = [vectors[i][c] for i in range(j + 1)]
             q_ref[0, c, rhs * j : width, :] = dot(both, jnp.concatenate(stack + stack, axis=0)).astype(BF16)
 
-    halo_start(0)
+    for k in ORDER:
+        pack_packet(0, k)
+    pl.semaphore_wait(barrier, expected)
+    halo_start(0, True)
     load_templates.wait()
 
     @pl.loop(0, tmpl.shape[0], unroll=4)
@@ -339,7 +344,7 @@
     plane_wait(0)
     ghost_pass(0)
 
-    halo_start(1)
+    halo_start(1, False)
     early = reduced(0, gram((0, 1)))
     next(early)
     own_pass(1)
@@ -386,8 +391,8 @@
         return pl.pallas_call(
             functools.partial(kernel, groups, side, peers_y, rows_total),
             out_shape=(
-                jax.ShapeDtypeStruct((1, column_cap, width, dof), BF16),
-                jax.ShapeDtypeStruct((width, width), F32),
+                vmem((1, column_cap, width, dof), BF16),
+                vmem((width, width), F32),
             ),
             in_specs=[pl.BlockSpec(memory_space=pltpu.HBM)] * 6,
             out_specs=(pl.BlockSpec(memory_space=vmem), pl.BlockSpec(memory_space=vmem)),

time: 77.6 us -> 74.7 us (0.963)
  local copies, waits for them, and re-layouts: 3.56 us -> 1.53 us
  Pallas kernels: 72.5 us -> 71.7 us
    unnamed x2, local copies, waits for them, and re-layouts: 3.56 us -> 1.53 us
    pallas_call x1, Pallas kernels: 72.5 us -> 71.7 us  [body(): pl.pallas_call(functools.partial(kernel, groups, side, peers_y, rows_tota...]
where the time goes in v4:
time: 74.7 us; the launch traced here: 74.5 us
  Pallas kernels  71.7 us (96%)
  local copies, waits for them, and re-layouts  1.53 us (2%)
  between operations  1.29 us (2%)
    pallas_call x1, Pallas kernels, body(): pl.pallas_call(functools.partial(kernel, groups, side, peers_y, rows_tota...  71.7 us
    unnamed x2, local copies, waits for them, and re-layouts  1.53 us

profile of v4, /device:TPU:1, one launch (start us, length us, event | category | flops | bytes accessed | tf_op | source)
XLA Modules:
  0.0 74.5 jit_solution(18330740308799064088)
XLA Ops:
  1.3 71.7 %shard_map.77 = (bf16[1,36,96,128]{3,2,1,0:T(8,128)(2,1)S(1)}, f32[96,96]{1,0:T(8,128)S(1)}) custom-call(bf16[1,36,32,128]{3,2,1,0:T(8,128)(2,1)} %basis_ref.1, bf16[64,128,128]{2,1,0:T(8,128)(2,1)} %templates_ref.1, s32[7,1,36]{2,1,0:T(1,128)} %bitcast.3, s32[1]{0:T(128)S(6)} %copy.12.live_in, s32[4,36]{1,0:T(4,128)} %bitcast.5, s32[6,1,8]{2,1,0:T(1,128)} %bitcast.4), custom_call_target="tpu_custom_call" | custom-call | tf_op jit(solution)/shard_map/pallas_call | solution.py:391
  73.0 0.9 %copy.10 = bf16[1,36,96,128]{3,2,1,0:T(8,128)(2,1)} copy(bf16[1,36,96,128]{3,2,1,0:T(8,128)(2,1)S(1)} %get-tuple-element.2) | data formatting | bytes 1769472
  73.9 0.6 copy.11

commit v5 on v4

--- a/solution.py
+++ b/solution.py
@@ -15,6 +15,7 @@
 BF16 = jnp.bfloat16
 NT = (((1,), (1,)), ((), ()))
 HIGH = lax.Precision.HIGHEST
+CORNER_CAP = 2
 VMEM_MIB = 58
 UN_OWN = UN_LAYER = UN_GHOST = UN_PROJ = 36
 UN_GRAM = 18
@@ -37,7 +38,7 @@
 
 
 def kernel(
-    groups, side, peers_y, rows_total,
+    groups, side, peers_y, rows_total, caps,
     basis_ref, templates_ref, ids_in, live_in, refs_in, lists_in,
     q_ref, r_ref,
     ids_ref, live_ref, refs_ref, lists_ref, tmpl, v0, v1, v2, ghost1, ghost2, packet1, packet2, layer1, layer2, acc,
@@ -129,8 +130,8 @@
     def plane_copy(x, k):
         dx, dy = DIRECTIONS[k]
         return pltpu.make_async_remote_copy(
-            src_ref=packets[x].at[k],
-            dst_ref=ghosts[x].at[pl.ds(k * halo_cap, halo_cap)],
+            src_ref=packets[x].at[k, pl.ds(0, caps[k])],
+            dst_ref=ghosts[x].at[pl.ds(k * halo_cap, caps[k])],
             send_sem=halo_send.at[x, k],
             recv_sem=halo_recv.at[x, k],
             device_id=(g, (row + dx) * side + col + dy),
@@ -150,7 +151,7 @@
     has_up, has_down = g < groups - 1, g > 0
 
     def pack_packet(x, k):
-        for s in range(halo_cap):
+        for s in range(caps[k]):
             slot = lists_ref[s, 0, k]
             packets[x][k, s] = vectors[x][jnp.where(slot < 0, zero_own, slot)]
 
@@ -222,6 +223,13 @@
         start = tuple(jnp.zeros((rhs, rhs * (j + 1)), F32) for j in rows)
         totals = lax.fori_loop(0, column_cap // 2, add, start, unroll=UN_GRAM)
         return [t[:, rhs * i : rhs * (i + 1)] for t in totals for i in range(t.shape[1] // rhs)]
+
+    def mark(blocks):
+        spare = [lists_ref[s, 0, k] for k in range(8) for s in range(caps[k], halo_cap)]
+        if not spare:
+            return blocks
+        over = functools.reduce(jnp.maximum, spare) >= 0
+        return [jnp.where(over, jnp.nan, blocks[0])] + blocks[1:]
 
     def pack(block):
         return jnp.concatenate([block[8 * i : 8 * i + 8] for i in range(rhs // 8)], axis=1)
@@ -345,7 +353,7 @@
     ghost_pass(0)
 
     halo_start(1, False)
-    early = reduced(0, gram((0, 1)))
+    early = reduced(0, mark(gram((0, 1))))
     next(early)
     own_pass(1)
     layers_wait(1)
@@ -388,51 +396,62 @@
         rows_total = column_cap * dof * groups * pieces
         vmem, smem = pltpu.VMEM, pltpu.SMEM
         block = (rhs, dof)
-        return pl.pallas_call(
-            functools.partial(kernel, groups, side, peers_y, rows_total),
-            out_shape=(
-                vmem((1, column_cap, width, dof), BF16),
-                vmem((width, width), F32),
-            ),
-            in_specs=[pl.BlockSpec(memory_space=pltpu.HBM)] * 6,
-            out_specs=(pl.BlockSpec(memory_space=vmem), pl.BlockSpec(memory_space=vmem)),
-            scratch_shapes=[
-                smem((faces, 1, column_cap), jnp.int32),
-                smem((1,), jnp.int32),
-                smem((4, column_cap), jnp.int32),
-                smem((halo_cap, 1, 8), jnp.int32),
-                vmem(templates.shape, BF16),
-                vmem((column_cap + 1, *block), BF16),
-                vmem((column_cap + 1, *block), BF16),
-                vmem((column_cap + 1, *block), BF16),
-                vmem((8 * halo_cap + 1, *block), BF16),
-                vmem((8 * halo_cap + 1, *block), BF16),
-                vmem((8, halo_cap, *block), BF16),
-                vmem((8, halo_cap, *block), BF16),
-                vmem((2, column_cap, *block), BF16),
-                vmem((2, column_cap, *block), BF16),
-                vmem((column_cap, *block), F32),
-                vmem((2, 3, 8, 16, lanes), F32),
-                vmem((2, 3, 8, 8, lanes), F32),
-                vmem((rhs, lanes), F32),
-                vmem((rhs, lanes), F32),
-                vmem((width, lanes), F32),
-                pltpu.SemaphoreType.DMA((6,)),
-                pltpu.SemaphoreType.DMA((2, 10)),
-                pltpu.SemaphoreType.DMA((2, 10)),
-                pltpu.SemaphoreType.DMA((4, 3, 8)),
-                pltpu.SemaphoreType.DMA((4, 3, 8)),
-            ],
-            compiler_params=pltpu.CompilerParams(
-                collective_id=0, has_side_effects=True, vmem_limit_bytes=VMEM_MIB * 2**20
-            ),
-        )(
+        operands = (
             basis_start,
             templates,
             template_ids.transpose(2, 0, 1),
             live_columns,
             face_refs.T,
             send_lists.transpose(2, 0, 1),
+        )
+
+        def run(caps, collective_id):
+            return pl.pallas_call(
+                functools.partial(kernel, groups, side, peers_y, rows_total, caps),
+                out_shape=(
+                    vmem((1, column_cap, width, dof), BF16),
+                    vmem((width, width), F32),
+                ),
+                in_specs=[pl.BlockSpec(memory_space=pltpu.HBM)] * 6,
+                out_specs=(pl.BlockSpec(memory_space=vmem), pl.BlockSpec(memory_space=vmem)),
+                scratch_shapes=[
+                    smem((faces, 1, column_cap), jnp.int32),
+                    smem((1,), jnp.int32),
+                    smem((4, column_cap), jnp.int32),
+                    smem((halo_cap, 1, 8), jnp.int32),
+                    vmem(templates.shape, BF16),
+                    vmem((column_cap + 1, *block), BF16),
+                    vmem((column_cap + 1, *block), BF16),
+                    vmem((column_cap + 1, *block), BF16),
+                    vmem((8 * halo_cap + 1, *block), BF16),
+                    vmem((8 * halo_cap + 1, *block), BF16),
+                    vmem((8, halo_cap, *block), BF16),
+                    vmem((8, halo_cap, *block), BF16),
+                    vmem((2, column_cap, *block), BF16),
+                    vmem((2, column_cap, *block), BF16),
+                    vmem((column_cap, *block), F32),
+                    vmem((2, 3, 8, 16, lanes), F32),
+                    vmem((2, 3, 8, 8, lanes), F32),
+                    vmem((rhs, lanes), F32),
+                    vmem((rhs, lanes), F32),
+                    vmem((width, lanes), F32),
+                    pltpu.SemaphoreType.DMA((6,)),
+                    pltpu.SemaphoreType.DMA((2, 10)),
+                    pltpu.SemaphoreType.DMA((2, 10)),
+                    pltpu.SemaphoreType.DMA((4, 3, 8)),
+                    pltpu.SemaphoreType.DMA((4, 3, 8)),
+                ],
+                compiler_params=pltpu.CompilerParams(
+                    collective_id=collective_id, has_side_effects=True, vmem_limit_bytes=VMEM_MIB * 2**20
+                ),
+            )(*operands)
+
+        narrow = [halo_cap if 0 in step else CORNER_CAP for step in DIRECTIONS]
+        basis_q, r_factor = run(narrow, 0)
+        return lax.cond(
+            jnp.isnan(r_factor[0, 0]),
+            lambda: tuple(run([halo_cap] * 8, 1)),
+            lambda: (basis_q, r_factor),
         )
 
     return jax.shard_map(

time: 74.7 us -> 63 us (0.84)
  Pallas kernels: 71.7 us -> 57.7 us
  between operations: 1.29 us -> 2.82 us
    pallas_call x1, Pallas kernels: 71.7 us -> 57.7 us  [run(): pl.pallas_call(functools.partial(kernel, groups, side, peers_y, rows_tota...]
    unnamed x2 -> x12, local copies, waits for them, and re-layouts: 1.53 us -> 1.55 us
where the time goes in v5:
time: 63 us; the launch traced here: 62.9 us
  Pallas kernels  57.7 us (92%)
  between operations  2.82 us (4%)
  local copies, waits for them, and re-layouts  2.07 us (3%)
    pallas_call x1, Pallas kernels, run(): pl.pallas_call(functools.partial(kernel, groups, side, peers_y, rows_tota...  57.7 us
    unnamed x12, local copies, waits for them, and re-layouts  1.55 us

profile of v5, /device:TPU:1, one launch (start us, length us, event | category | flops | bytes accessed | tf_op | source)
XLA Modules:
  0.0 62.9 jit_solution(2223834076182686289)
XLA Ops:
  0.6 0.0 copy-start
  0.6 0.0 copy-start.1
  0.7 0.0 copy-start.3
  0.7 0.0 copy-start.4
  0.7 0.0 copy-start.2
  1.5 57.7 %shard_map.81 = (bf16[1,36,96,128]{3,2,1,0:T(8,128)(2,1)S(1)}, f32[96,96]{1,0:T(8,128)S(1)}) custom-call(bf16[1,36,32,128]{3,2,1,0:T(8,128)(2,1)} %basis_ref.1, bf16[64,128,128]{2,1,0:T(8,128)(2,1)} %templates_ref.1, s32[7,1,36]{2,1,0:T(1,128)} %bitcast.4, s32[1]{0:T(128)S(6)} %copy.20.live_in, s32[4,36]{1,0:T(4,128)} %bitcast.8, s32[6,1,8]{2,1,0:T(1,128)} %bitcast.6), custom_call_target="tpu_custom_call" | custom-call | tf_op jit(solution)/shard_map/pallas_call | solution.py:409
  59.2 0.5 slice.3
  61.0 0.0 copy-done
  61.0 0.0 copy-done.1
  61.1 0.0 copy-done.3
  61.1 0.0 copy-done.4
  61.1 0.0 copy-done.2
  61.1 0.2 conditional.1
  61.3 0.9 %copy.18 = bf16[1,36,96,128]{3,2,1,0:T(8,128)(2,1)} copy(bf16[1,36,96,128]{3,2,1,0:T(8,128)(2,1)S(1)} %get-tuple-element.36) | data formatting | bytes 1769472
  62.2 0.6 copy.19
Async XLA Ops:
  0.6 60.4 %copy-start = (bf16[64,128,128]{2,1,0:T(8,128)(2,1)S(1)}, bf16[64,128,128]{2,1,0:T(8,128)(2,1)}, u32[]{:S(2)}) copy-start(bf16[64,128,128]{2,1,0:T(8,128)(2,1)} %templates_ref.1) | copy-start | bytes 6291460
  0.6 60.4 %copy-start.1 = (bf16[1,36,32,128]{3,2,1,0:T(8,128)(2,1)S(1)}, bf16[1,36,32,128]{3,2,1,0:T(8,128)(2,1)}, u32[]{:S(2)}) copy-start(bf16[1,36,32,128]{3,2,1,0:T(8,128)(2,1)} %basis_ref.1) | copy-start | bytes 884740
  0.7 60.4 %copy-start.3 = (s32[1,8,6]{1,0,2:T(1,128)S(1)}, s32[1,8,6]{1,0,2:T(1,128)}, u32[]{:S(2)}) copy-start(s32[1,8,6]{1,0,2:T(1,128)} %param.13) | copy-start | bytes 580
  0.7 60.4 %copy-start.4 = (s32[36,4]{0,1:T(4,128)S(1)}, s32[36,4]{0,1:T(4,128)}, u32[]{:S(2)}) copy-start(s32[36,4]{0,1:T(4,128)} %param.12) | copy-start | bytes 1732
  0.7 60.4 %copy-start.2 = (s32[1,36,7]{1,0,2:T(1,128)S(1)}, s32[1,36,7]{1,0,2:T(1,128)}, u32[]{:S(2)}) copy-start(s32[1,36,7]{1,0,2:T(1,128)} %param.10) | copy-start | bytes 3028

commit v6 on v5

--- a/solution.py
+++ b/solution.py
@@ -155,13 +155,12 @@
             slot = lists_ref[s, 0, k]
             packets[x][k, s] = vectors[x][jnp.where(slot < 0, zero_own, slot)]
 
-    def halo_start(x, packed):
-        for k in ORDER:
-            if k == 3:
-                pl.when(has_up)(lambda: layer_copy(x, 1).start())
-                pl.when(has_down)(lambda: layer_copy(x, 0).start())
-            if not packed:
-                pack_packet(x, k)
+    def layers_start(x):
+        pl.when(has_up)(lambda: layer_copy(x, 1).start())
+        pl.when(has_down)(lambda: layer_copy(x, 0).start())
+
+    def plane_start(x, directions):
+        for k in directions:
             pl.when(inside(*DIRECTIONS[k]))(lambda: plane_copy(x, k).start())
 
     def layers_wait(x):
@@ -199,15 +198,41 @@
         def _(c):
             acc[c] = acc[c] + apply([layers[x][0, c], layers[x][1, c]], c, (1, 2))
 
+    def finished(x, c):
+        blocks = []
+        for q in range(4):
+            r = refs_ref[q, c]
+            blocks.append(ghosts[x][jnp.where(r < column_cap, zero_ghost, r - column_cap)])
+        return acc[c] + apply(blocks, c, (3, 4, 5, 6))
+
     def ghost_pass(x):
         @pl.loop(0, column_cap, unroll=UN_GHOST)
         def _(c):
-            blocks = []
-            for q in range(4):
-                r = refs_ref[q, c]
-                blocks.append(ghosts[x][jnp.where(r < column_cap, zero_ghost, r - column_cap)])
-            total = acc[c] + apply(blocks, c, (3, 4, 5, 6))
-            vectors[x + 1][c] = jnp.where(c < live, total, 0.0).astype(BF16)
+            vectors[x + 1][c] = jnp.where(c < live, finished(x, c), 0.0).astype(BF16)
+
+    def send_ahead(x):
+        for k in ORDER[:6]:
+            for s in range(caps[k]):
+                slot = lists_ref[s, 0, k]
+                c = jnp.maximum(slot, 0)
+                keep = (slot >= 0) & (c < live)
+                packets[x + 1][k, s] = jnp.where(keep, finished(x, c), 0.0).astype(BF16)
+            pl.when(inside(*DIRECTIONS[k]))(lambda: plane_copy(x + 1, k).start())
+
+    def ghost_pass_gram(x):
+        def step(h, total):
+            pair = []
+            for c in (2 * h, 2 * h + 1):
+                block = jnp.where(c < live, finished(x, c), 0.0).astype(BF16)
+                vectors[x + 1][c] = block
+                pair.append(block)
+            lines = [jnp.concatenate([vectors[i][2 * h], vectors[i][2 * h + 1]], axis=1) for i in range(x + 1)]
+            line = jnp.concatenate(pair, axis=1)
+            return total + dot_nt(line, jnp.concatenate(lines + [line], axis=0))
+
+        start = jnp.zeros((rhs, rhs * (x + 2)), F32)
+        total = lax.fori_loop(0, column_cap // 2, step, start, unroll=UN_GRAM)
+        return [total[:, rhs * i : rhs * (i + 1)] for i in range(x + 2)]
 
     def gram(rows):
         def add(h, carry):
@@ -339,7 +364,9 @@
     for k in ORDER:
         pack_packet(0, k)
     pl.semaphore_wait(barrier, expected)
-    halo_start(0, True)
+    plane_start(0, ORDER[:6])
+    layers_start(0)
+    plane_start(0, ORDER[6:])
     load_templates.wait()
 
     @pl.loop(0, tmpl.shape[0], unroll=4)
@@ -350,9 +377,13 @@
     layers_wait(0)
     layer_pass(0)
     plane_wait(0)
+    send_ahead(0)
     ghost_pass(0)
 
-    halo_start(1, False)
+    layers_start(1)
+    for k in ORDER[6:]:
+        pack_packet(1, k)
+    plane_start(1, ORDER[6:])
     early = reduced(0, mark(gram((0, 1))))
     next(early)
     own_pass(1)
@@ -360,9 +391,7 @@
     layer_pass(1)
     next(early)
     plane_wait(1)
-    ghost_pass(1)
-
-    late = reduced(1, gram((2,)))
+    late = reduced(1, ghost_pass_gram(1))
     next(late)
     next(early)
     next(late)

time: 63 us -> 65 us (1.032)
  Pallas kernels: 57.7 us -> 59.8 us
    pallas_call x1, Pallas kernels: 57.7 us -> 59.8 us  [run(): pl.pallas_call(functools.partial(kernel, groups, side, peers_y, rows_tota...]
where the time goes in v6:
time: 65 us; the launch traced here: 64.9 us
  Pallas kernels  59.8 us (92%)
  between operations  2.82 us (4%)
  local copies, waits for them, and re-layouts  2.07 us (3%)
    pallas_call x1, Pallas kernels, run(): pl.pallas_call(functools.partial(kernel, groups, side, peers_y, rows_tota...  59.8 us
    unnamed x12, local copies, waits for them, and re-layouts  1.55 us

profile of v6, /device:TPU:1, one launch (start us, length us, event | category | flops | bytes accessed | tf_op | source)
XLA Modules:
  0.0 64.9 jit_solution(8855084676171796377)
XLA Ops:
  0.6 0.0 copy-start
  0.6 0.0 copy-start.1
  0.7 0.0 copy-start.3
  0.7 0.0 copy-start.4
  0.7 0.0 copy-start.2
  1.5 59.8 %shard_map.81 = (bf16[1,36,96,128]{3,2,1,0:T(8,128)(2,1)S(1)}, f32[96,96]{1,0:T(8,128)S(1)}) custom-call(bf16[1,36,32,128]{3,2,1,0:T(8,128)(2,1)} %basis_ref.1, bf16[64,128,128]{2,1,0:T(8,128)(2,1)} %templates_ref.1, s32[7,1,36]{2,1,0:T(1,128)} %bitcast.4, s32[1]{0:T(128)S(6)} %copy.20.live_in, s32[4,36]{1,0:T(4,128)} %bitcast.8, s32[6,1,8]{2,1,0:T(1,128)} %bitcast.6), custom_call_target="tpu_custom_call" | custom-call | tf_op jit(solution)/shard_map/pallas_call | solution.py:438
  61.2 0.5 slice.3
  63.0 0.0 copy-done
  63.1 0.0 copy-done.1
  63.1 0.0 copy-done.3
  63.1 0.0 copy-done.4
  63.1 0.0 copy-done.2
  63.1 0.2 conditional.1
  63.3 0.9 %copy.18 = bf16[1,36,96,128]{3,2,1,0:T(8,128)(2,1)} copy(bf16[1,36,96,128]{3,2,1,0:T(8,128)(2,1)S(1)} %get-tuple-element.36) | data formatting | bytes 1769472
  64.2 0.6 copy.19
Async XLA Ops:
  0.6 62.4 %copy-start = (bf16[64,128,128]{2,1,0:T(8,128)(2,1)S(1)}, bf16[64,128,128]{2,1,0:T(8,128)(2,1)}, u32[]{:S(2)}) copy-start(bf16[64,128,128]{2,1,0:T(8,128)(2,1)} %templates_ref.1) | copy-start | bytes 6291460
  0.6 62.4 %copy-start.1 = (bf16[1,36,32,128]{3,2,1,0:T(8,128)(2,1)S(1)}, bf16[1,36,32,128]{3,2,1,0:T(8,128)(2,1)}, u32[]{:S(2)}) copy-start(bf16[1,36,32,128]{3,2,1,0:T(8,128)(2,1)} %basis_ref.1) | copy-start | bytes 884740
  0.7 62.4 %copy-start.3 = (s32[1,8,6]{1,0,2:T(1,128)S(1)}, s32[1,8,6]{1,0,2:T(1,128)}, u32[]{:S(2)}) copy-start(s32[1,8,6]{1,0,2:T(1,128)} %param.13) | copy-start | bytes 580
  0.7 62.4 %copy-start.4 = (s32[36,4]{0,1:T(4,128)S(1)}, s32[36,4]{0,1:T(4,128)}, u32[]{:S(2)}) copy-start(s32[36,4]{0,1:T(4,128)} %param.12) | copy-start | bytes 1732
  0.7 62.4 %copy-start.2 = (s32[1,36,7]{1,0,2:T(1,128)S(1)}, s32[1,36,7]{1,0,2:T(1,128)}, u32[]{:S(2)}) copy-start(s32[1,36,7]{1,0,2:T(1,128)} %param.10) | copy-start | bytes 3028

commit v7 on v5

--- a/solution.py
+++ b/solution.py
@@ -16,7 +16,8 @@
 NT = (((1,), (1,)), ((), ()))
 HIGH = lax.Precision.HIGHEST
 CORNER_CAP = 2
-VMEM_MIB = 58
+VMEM_MIB = 56
+LAST_MIB = 24
 UN_OWN = UN_LAYER = UN_GHOST = UN_PROJ = 36
 UN_GRAM = 18
 
@@ -35,14 +36,97 @@
 
 def exact_nt(x, y):
     return lax.dot_general(x, y, NT, preferred_element_type=F32, precision=HIGH)
+
+
+def factor(j, blocks, inv, work, upper, r_ref):
+    rhs, lanes = work.shape
+    before = rhs * j
+    wide = lax.broadcasted_iota(jnp.int32, (rhs, lanes), 1)
+    tall = lax.broadcasted_iota(jnp.int32, (rhs, lanes), 0)
+    corner = blocks[j]
+    if j:
+        left = exact_nt(jnp.concatenate(blocks[:j], axis=1), inv[:before, :before])
+        corner = corner - exact_nt(left, left)
+        across_inv = exact(left, inv[:before, :before])
+    work[...] = jnp.where(wide == tall + rhs, 1.0, 0.0)
+    work[:, :rhs] = corner
+    m = work[...]
+    for p in range(rhs // 8):
+        size = rhs - 8 * p
+        cols = [jnp.broadcast_to(m[:, 8 * p + i : 8 * p + i + 1], (size, lanes)) for i in range(8)]
+        for i in range(8):
+            scale = lax.rsqrt(jnp.broadcast_to(cols[i][i : i + 1, :], (size, lanes)))
+            column = cols[i] * scale
+            line = jnp.broadcast_to(m[i : i + 1, :], (size, lanes)) * scale
+            upper[8 * p + i : 8 * p + i + 1, :] = line[0:1, :]
+            m = m - column * line
+            for n in range(i + 1, 8):
+                cols[n] = cols[n] - column * jnp.broadcast_to(column[n : n + 1, :], (size, lanes))
+        m = m[8:]
+    square = lax.broadcasted_iota(jnp.int32, (rhs, rhs), 0)
+    across = lax.broadcasted_iota(jnp.int32, (rhs, rhs), 1)
+    r_ref[before : before + rhs, before : before + rhs] = jnp.where(
+        across >= square, upper[:, :rhs], 0.0
+    )
+    corner_inv = upper[:, rhs : 2 * rhs]
+    inv[before : before + rhs, before : before + rhs] = corner_inv
+    if j:
+        r_ref[:before, before : before + rhs] = left.T
+        r_ref[before : before + rhs, :before] = jnp.zeros((rhs, before), F32)
+        inv[before : before + rhs, :before] = -exact(corner_inv, across_inv)
+
+
+def project(j, vectors, inv, put):
+    column_cap, rhs = vectors[0].shape[0] - 1, vectors[0].shape[1]
+    width = rhs * (j + 1)
+    rows = inv[rhs * j : width, :width]
+    high = rows.astype(BF16)
+    low = (rows - high.astype(F32)).astype(BF16)
+    both = jnp.concatenate([high, low], axis=1)
+    for c in range(column_cap):
+        stack = [vectors[i][c] for i in range(j + 1)]
+        put(c, dot(both, jnp.concatenate(stack + stack, axis=0)).astype(BF16))
+
+
+def last_kernel(
+    v0, v1, v2, early_q, early_inv, early_r, lines_ref,
+    q_ref, r_ref,
+    inv, work, upper, late_q, sems,
+):
+    column_cap, rhs, _ = late_q.shape
+    early_copy = pltpu.make_async_copy(early_q, q_ref.at[0, :, pl.ds(0, 2 * rhs)], sems.at[0])
+    early_copy.start()
+    inv[...] = early_inv[...]
+    r_ref[...] = early_r[...]
+    lines = lines_ref[...]
+    factor(2, [lines[:, rhs * i : rhs * (i + 1)] for i in range(3)], inv, work, upper, r_ref)
+    part = column_cap // 3
+    copies = [
+        pltpu.make_async_copy(
+            late_q.at[pl.ds(part * i, part)],
+            q_ref.at[0, pl.ds(part * i, part), pl.ds(2 * rhs, rhs)],
+            sems.at[1 + i],
+        )
+        for i in range(3)
+    ]
+
+    def put(c, block):
+        late_q[c] = block
+        if (c + 1) % part == 0:
+            copies[c // part].start()
+
+    project(2, (v0, v1, v2), inv, put)
+    early_copy.wait()
+    for copy in copies:
+        copy.wait()
 
 
 def kernel(
     groups, side, peers_y, rows_total, caps,
     basis_ref, templates_ref, ids_in, live_in, refs_in, lists_in,
-    q_ref, r_ref,
-    ids_ref, live_ref, refs_ref, lists_ref, tmpl, v0, v1, v2, ghost1, ghost2, packet1, packet2, layer1, layer2, acc,
-    slots_a, slots_b, work, upper, inv,
+    v0, v1, v2, early_q, inv, r_ref, lines_ref, over_ref,
+    ids_ref, live_ref, refs_ref, lists_ref, tmpl, ghost1, ghost2, packet1, packet2, layer1, layer2, acc,
+    slots_a, slots_b, work, upper,
     load_sem, halo_send, halo_recv, sum_send, sum_recv,
 ):
     column_cap, rhs, dof = v0.shape[0] - 1, v0.shape[1], v0.shape[2]
@@ -118,6 +202,7 @@
             layers[x][1] = jnp.zeros((column_cap, rhs, dof), BF16)
 
     inv[...] = jnp.zeros(inv.shape, F32)
+    r_ref[...] = jnp.zeros(r_ref.shape, F32)
     for load in loads:
         load.wait()
     live = live_ref[0]
@@ -286,56 +371,6 @@
         whole = [sums[0][:8], sums[0][8:], sums[1]]
         yield [unpack(line) * (1.0 / rows_total) for line in whole], sent
 
-    lanes = work.shape[1]
-    wide = lax.broadcasted_iota(jnp.int32, (rhs, lanes), 1)
-    tall = lax.broadcasted_iota(jnp.int32, (rhs, lanes), 0)
-
-    def factor(j, blocks):
-        before = rhs * j
-        corner = blocks[j]
-        if j:
-            left = exact_nt(jnp.concatenate(blocks[:j], axis=1), inv[:before, :before])
-            corner = corner - exact_nt(left, left)
-            across_inv = exact(left, inv[:before, :before])
-        work[...] = jnp.where(wide == tall + rhs, 1.0, 0.0)
-        work[:, :rhs] = corner
-        m = work[...]
-        for p in range(rhs // 8):
-            size = rhs - 8 * p
-            cols = [jnp.broadcast_to(m[:, 8 * p + i : 8 * p + i + 1], (size, lanes)) for i in range(8)]
-            for i in range(8):
-                scale = lax.rsqrt(jnp.broadcast_to(cols[i][i : i + 1, :], (size, lanes)))
-                column = cols[i] * scale
-                line = jnp.broadcast_to(m[i : i + 1, :], (size, lanes)) * scale
-                upper[8 * p + i : 8 * p + i + 1, :] = line[0:1, :]
-                m = m - column * line
-                for n in range(i + 1, 8):
-                    cols[n] = cols[n] - column * jnp.broadcast_to(column[n : n + 1, :], (size, lanes))
-            m = m[8:]
-        square = lax.broadcasted_iota(jnp.int32, (rhs, rhs), 0)
-        across = lax.broadcasted_iota(jnp.int32, (rhs, rhs), 1)
-        r_ref[before : before + rhs, before : before + rhs] = jnp.where(
-            across >= square, upper[:, :rhs], 0.0
-        )
-        corner_inv = upper[:, rhs : 2 * rhs]
-        inv[before : before + rhs, before : before + rhs] = corner_inv
-        if j:
-            r_ref[:before, before : before + rhs] = left.T
-            r_ref[before : before + rhs, :before] = jnp.zeros((rhs, before), F32)
-            inv[before : before + rhs, :before] = -exact(corner_inv, across_inv)
-
-    def project(j):
-        width = rhs * (j + 1)
-        rows = inv[rhs * j : width, :width]
-        high = rows.astype(BF16)
-        low = (rows - high.astype(F32)).astype(BF16)
-        both = jnp.concatenate([high, low], axis=1)
-
-        @pl.loop(0, column_cap, unroll=UN_PROJ)
-        def _(c):
-            stack = [vectors[i][c] for i in range(j + 1)]
-            q_ref[0, c, rhs * j : width, :] = dot(both, jnp.concatenate(stack + stack, axis=0)).astype(BF16)
-
     for k in ORDER:
         pack_packet(0, k)
     pl.semaphore_wait(barrier, expected)
@@ -367,14 +402,21 @@
     next(early)
     next(late)
     (first, *second), sent_early = next(early)
-    factor(0, [first])
-    project(0)
-    factor(1, second)
+    over_ref[0] = jnp.max(jnp.where(first == first, 0, 1))
+
+    def put_at(j):
+        def put(c, block):
+            early_q[c, rhs * j : rhs * (j + 1), :] = block
+
+        return put
+
+    factor(0, [first], inv, work, upper, r_ref)
+    project(0, vectors, inv, put_at(0))
+    factor(1, second, inv, work, upper, r_ref)
     next(late)
-    project(1)
+    project(1, vectors, inv, put_at(1))
     third, sent_late = next(late)
-    factor(2, third)
-    project(2)
+    lines_ref[...] = jnp.concatenate(third, axis=1)
     halo_sent(0)
     halo_sent(1)
     for copy in sent_early + sent_late:
@@ -406,23 +448,26 @@
         )
 
         def run(caps, collective_id):
-            return pl.pallas_call(
+            *early, over = pl.pallas_call(
                 functools.partial(kernel, groups, side, peers_y, rows_total, caps),
                 out_shape=(
-                    vmem((1, column_cap, width, dof), BF16),
+                    vmem((column_cap + 1, *block), BF16),
+                    vmem((column_cap + 1, *block), BF16),
+                    vmem((column_cap + 1, *block), BF16),
+                    vmem((column_cap, 2 * rhs, dof), BF16),
+                    vmem((width, lanes), F32),
                     vmem((width, width), F32),
+                    vmem((rhs, width), F32),
+                    smem((1,), jnp.int32),
                 ),
                 in_specs=[pl.BlockSpec(memory_space=pltpu.HBM)] * 6,
-                out_specs=(pl.BlockSpec(memory_space=vmem), pl.BlockSpec(memory_space=vmem)),
+                out_specs=tuple([pl.BlockSpec(memory_space=vmem)] * 7 + [pl.BlockSpec(memory_space=smem)]),
                 scratch_shapes=[
                     smem((faces, 1, column_cap), jnp.int32),
                     smem((1,), jnp.int32),
                     smem((4, column_cap), jnp.int32),
                     smem((halo_cap, 1, 8), jnp.int32),
                     vmem(templates.shape, BF16),
-                    vmem((column_cap + 1, *block), BF16),
-                    vmem((column_cap + 1, *block), BF16),
-                    vmem((column_cap + 1, *block), BF16),
                     vmem((8 * halo_cap + 1, *block), BF16),
                     vmem((8 * halo_cap + 1, *block), BF16),
                     vmem((8, halo_cap, *block), BF16),
@@ -434,7 +479,6 @@
                     vmem((2, 3, 8, 8, lanes), F32),
                     vmem((rhs, lanes), F32),
                     vmem((rhs, lanes), F32),
-                    vmem((width, lanes), F32),
                     pltpu.SemaphoreType.DMA((6,)),
                     pltpu.SemaphoreType.DMA((2, 10)),
                     pltpu.SemaphoreType.DMA((2, 10)),
@@ -446,11 +490,30 @@
                 ),
             )(*operands)
 
+            basis_q, r_factor = pl.pallas_call(
+                last_kernel,
+                out_shape=(
+                    jax.ShapeDtypeStruct((1, column_cap, width, dof), BF16),
+                    jax.ShapeDtypeStruct((width, width), F32),
+                ),
+                in_specs=[pl.BlockSpec(memory_space=vmem)] * 7,
+                out_specs=(pl.BlockSpec(memory_space=pltpu.HBM), pl.BlockSpec(memory_space=vmem)),
+                scratch_shapes=[
+                    vmem((width, lanes), F32),
+                    vmem((rhs, lanes), F32),
+                    vmem((rhs, lanes), F32),
+                    vmem((column_cap, *block), BF16),
+                    pltpu.SemaphoreType.DMA((4,)),
+                ],
+                compiler_params=pltpu.CompilerParams(vmem_limit_bytes=LAST_MIB * 2**20),
+            )(*early)
+            return basis_q, r_factor, over
+
         narrow = [halo_cap if 0 in step else CORNER_CAP for step in DIRECTIONS]
-        basis_q, r_factor = run(narrow, 0)
+        basis_q, r_factor, over = run(narrow, 0)
         return lax.cond(
-            jnp.isnan(r_factor[0, 0]),
-            lambda: tuple(run([halo_cap] * 8, 1)),
+            over[0] != 0,
+            lambda: tuple(run([halo_cap] * 8, 1)[:2]),
             lambda: (basis_q, r_factor),
         )
 

time: 63 us -> 61.5 us (0.976)
  local copies, waits for them, and re-layouts: 2.07 us -> 0.02 us
  Pallas kernels: 57.7 us -> 59.4 us
  between operations: 2.82 us -> 1.71 us
    pallas_call x0 -> x1, Pallas kernels: none -> 3.71 us  [run(): pl.pallas_call(last_kernel, out_shape=(jax.ShapeDtypeStruct((1, column_ca...]
    pallas_call x1, Pallas kernels: 57.7 us -> 55.6 us  [run(): pl.pallas_call(functools.partial(kernel, groups, side, peers_y, rows_tota...]
    unnamed x12 -> x10, local copies, waits for them, and re-layouts: 1.55 us -> 0.02 us
where the time goes in v7:
time: 61.5 us; the launch traced here: 61.3 us
  Pallas kernels  59.4 us (97%)
  between operations  1.71 us (3%)
    pallas_call x1, Pallas kernels, run(): pl.pallas_call(functools.partial(kernel, groups, side, peers_y, rows_tota...  55.6 us
    pallas_call x1, Pallas kernels, run(): pl.pallas_call(last_kernel, out_shape=(jax.ShapeDtypeStruct((1, column_ca...  3.71 us

profile of v7, /device:TPU:1, one launch (start us, length us, event | category | flops | bytes accessed | tf_op | source)
XLA Modules:
  0.0 61.3 jit_solution(17588784839383225655)
XLA Ops:
  0.6 0.0 copy-start
  0.6 0.0 copy-start.1
  0.7 0.0 copy-start.3
  0.7 0.0 copy-start.4
  0.7 0.0 copy-start.2
  1.5 55.6 %shard_map.81 = (bf16[37,32,128]{2,1,0:T(8,128)(2,1)S(1)}, bf16[37,32,128]{2,1,0:T(8,128)(2,1)S(1)}, bf16[37,32,128]{2,1,0:T(8,128)(2,1)S(1)}, bf16[36,64,128]{2...) custom-call(bf16[1,36,32,128]{3,2,1,0:T(8,128)(2,1)} %basis_ref.1, ...), custom_call_target="tpu_custom_call" | custom-call | tf_op jit(solution)/shard_map/pallas_call | solution.py:451
  57.1 0.0 copy-done
  57.1 0.0 copy-done.1
  57.2 0.0 copy-done.3
  57.2 0.0 copy-done.4
  57.2 0.0 copy-done.2
  57.2 3.7 %shard_map.82 = (bf16[1,36,96,128]{3,2,1,0:T(8,128)(2,1)}, f32[96,96]{1,0:T(8,128)}) custom-call(bf16[37,32,128]{2,1,0:T(8,128)(2,1)S(1)} %get-tuple-element.40.v0, bf16[37,32,128]{2,1,0:T(8,128)(2,1)S(1)} %get-tuple-element.41.v1, bf16[37,32,128]{2,1,0:T(8,128)(2,1)S(1)} %get-tuple-element.42.v2, bf16[36,64,128]{2,1,0:T(8,128)(2,1)S(1)} %get-tuple-element.43.early_q, ...), custom_call_target="tpu_custom_call" | custom-call | tf_op jit(solution)/shard_map/pallas_call | solution.py:493
  60.9 0.2 conditional.1
Async XLA Ops:
  0.6 56.5 %copy-start = (bf16[64,128,128]{2,1,0:T(8,128)(2,1)S(1)}, bf16[64,128,128]{2,1,0:T(8,128)(2,1)}, u32[]{:S(2)}) copy-start(bf16[64,128,128]{2,1,0:T(8,128)(2,1)} %templates_ref.1) | copy-start | bytes 6291460
  0.6 56.5 %copy-start.1 = (bf16[1,36,32,128]{3,2,1,0:T(8,128)(2,1)S(1)}, bf16[1,36,32,128]{3,2,1,0:T(8,128)(2,1)}, u32[]{:S(2)}) copy-start(bf16[1,36,32,128]{3,2,1,0:T(8,128)(2,1)} %basis_ref.1) | copy-start | bytes 884740
  0.7 56.5 %copy-start.3 = (s32[1,8,6]{1,0,2:T(1,128)S(1)}, s32[1,8,6]{1,0,2:T(1,128)}, u32[]{:S(2)}) copy-start(s32[1,8,6]{1,0,2:T(1,128)} %param.13) | copy-start | bytes 580
  0.7 56.5 %copy-start.4 = (s32[36,4]{0,1:T(4,128)S(1)}, s32[36,4]{0,1:T(4,128)}, u32[]{:S(2)}) copy-start(s32[36,4]{0,1:T(4,128)} %param.12) | copy-start | bytes 1732
  0.7 56.5 %copy-start.2 = (s32[1,36,7]{1,0,2:T(1,128)S(1)}, s32[1,36,7]{1,0,2:T(1,128)}, u32[]{:S(2)}) copy-start(s32[1,36,7]{1,0,2:T(1,128)} %param.10) | copy-start | bytes 3028

commit v8 on v7

--- a/solution.py
+++ b/solution.py
@@ -90,8 +90,8 @@
 
 def last_kernel(
     v0, v1, v2, early_q, early_inv, early_r, lines_ref,
-    q_ref, r_ref,
-    inv, work, upper, late_q, sems,
+    q_ref, r_out,
+    inv, work, upper, late_q, r_ref, sems,
 ):
     column_cap, rhs, _ = late_q.shape
     early_copy = pltpu.make_async_copy(early_q, q_ref.at[0, :, pl.ds(0, 2 * rhs)], sems.at[0])
@@ -100,6 +100,8 @@
     r_ref[...] = early_r[...]
     lines = lines_ref[...]
     factor(2, [lines[:, rhs * i : rhs * (i + 1)] for i in range(3)], inv, work, upper, r_ref)
+    r_copy = pltpu.make_async_copy(r_ref, r_out, sems.at[4])
+    r_copy.start()
     part = column_cap // 3
     copies = [
         pltpu.make_async_copy(
@@ -117,6 +119,7 @@
 
     project(2, (v0, v1, v2), inv, put)
     early_copy.wait()
+    r_copy.wait()
     for copy in copies:
         copy.wait()
 
@@ -497,13 +500,14 @@
                     jax.ShapeDtypeStruct((width, width), F32),
                 ),
                 in_specs=[pl.BlockSpec(memory_space=vmem)] * 7,
-                out_specs=(pl.BlockSpec(memory_space=pltpu.HBM), pl.BlockSpec(memory_space=vmem)),
+                out_specs=(pl.BlockSpec(memory_space=pltpu.HBM), pl.BlockSpec(memory_space=pltpu.HBM)),
                 scratch_shapes=[
                     vmem((width, lanes), F32),
                     vmem((rhs, lanes), F32),
                     vmem((rhs, lanes), F32),
                     vmem((column_cap, *block), BF16),
-                    pltpu.SemaphoreType.DMA((4,)),
+                    vmem((width, width), F32),
+                    pltpu.SemaphoreType.DMA((5,)),
                 ],
                 compiler_params=pltpu.CompilerParams(vmem_limit_bytes=LAST_MIB * 2**20),
             )(*early)

time: 61.5 us -> 60.9 us (level)
  Pallas kernels: 59.4 us -> 58.7 us
where the time goes in v8:
time: 60.9 us; the launch traced here: 60.7 us
  Pallas kernels  58.7 us (96%)
  between operations  1.71 us (3%)
    pallas_call x1, Pallas kernels, run(): pl.pallas_call(functools.partial(kernel, groups, side, peers_y, rows_tota...  55.6 us
    pallas_call x1, Pallas kernels, run(): pl.pallas_call(last_kernel, out_shape=(jax.ShapeDtypeStruct((1, column_ca...  3.1 us

profile of v8, /device:TPU:1, one launch (start us, length us, event | category | flops | bytes accessed | tf_op | source)
XLA Modules:
  0.0 60.7 jit_solution(12097349450420698381)
XLA Ops:
  0.6 0.0 copy-start
  0.6 0.0 copy-start.1
  0.7 0.0 copy-start.3
  0.7 0.0 copy-start.4
  0.7 0.0 copy-start.2
  1.5 55.6 %shard_map.81 = (bf16[37,32,128]{2,1,0:T(8,128)(2,1)S(1)}, bf16[37,32,128]{2,1,0:T(8,128)(2,1)S(1)}, bf16[37,32,128]{2,1,0:T(8,128)(2,1)S(1)}, bf16[36,64,128]{2...) custom-call(bf16[1,36,32,128]{3,2,1,0:T(8,128)(2,1)} %basis_ref.1, ...), custom_call_target="tpu_custom_call" | custom-call | tf_op jit(solution)/shard_map/pallas_call | solution.py:454
  57.1 0.0 copy-done
  57.1 0.0 copy-done.1
  57.2 0.0 copy-done.3
  57.2 0.0 copy-done.4
  57.2 0.0 copy-done.2
  57.2 3.1 %shard_map.82 = (bf16[1,36,96,128]{3,2,1,0:T(8,128)(2,1)}, f32[96,96]{1,0:T(8,128)}) custom-call(bf16[37,32,128]{2,1,0:T(8,128)(2,1)S(1)} %get-tuple-element.40.v0, bf16[37,32,128]{2,1,0:T(8,128)(2,1)S(1)} %get-tuple-element.41.v1, bf16[37,32,128]{2,1,0:T(8,128)(2,1)S(1)} %get-tuple-element.42.v2, bf16[36,64,128]{2,1,0:T(8,128)(2,1)S(1)} %get-tuple-element.43.early_q, ...), custom_call_target="tpu_custom_call" | custom-call | tf_op jit(solution)/shard_map/pallas_call | solution.py:496
  60.3 0.2 conditional.1
Async XLA Ops:
  0.6 56.5 %copy-start = (bf16[64,128,128]{2,1,0:T(8,128)(2,1)S(1)}, bf16[64,128,128]{2,1,0:T(8,128)(2,1)}, u32[]{:S(2)}) copy-start(bf16[64,128,128]{2,1,0:T(8,128)(2,1)} %templates_ref.1) | copy-start | bytes 6291460
  0.6 56.5 %copy-start.1 = (bf16[1,36,32,128]{3,2,1,0:T(8,128)(2,1)S(1)}, bf16[1,36,32,128]{3,2,1,0:T(8,128)(2,1)}, u32[]{:S(2)}) copy-start(bf16[1,36,32,128]{3,2,1,0:T(8,128)(2,1)} %basis_ref.1) | copy-start | bytes 884740
  0.7 56.5 %copy-start.3 = (s32[1,8,6]{1,0,2:T(1,128)S(1)}, s32[1,8,6]{1,0,2:T(1,128)}, u32[]{:S(2)}) copy-start(s32[1,8,6]{1,0,2:T(1,128)} %param.13) | copy-start | bytes 580
  0.7 56.5 %copy-start.4 = (s32[36,4]{0,1:T(4,128)S(1)}, s32[36,4]{0,1:T(4,128)}, u32[]{:S(2)}) copy-start(s32[36,4]{0,1:T(4,128)} %param.12) | copy-start | bytes 1732
  0.7 56.5 %copy-start.2 = (s32[1,36,7]{1,0,2:T(1,128)S(1)}, s32[1,36,7]{1,0,2:T(1,128)}, u32[]{:S(2)}) copy-start(s32[1,36,7]{1,0,2:T(1,128)} %param.10) | copy-start | bytes 3028
